TPU v7x, 32 devices: a whole 2x2x4 slice. The times are simulated.
32 devices in a mesh: dp: 2 (over core), context: 8 (over z, x), tensor: 2 (over y).
Axes of the slice: x: 2, y: 2, z: 4, core: 2. Of those that a mesh axis runs over, the one named last changes fastest.
Arguments:
- layer_input: bfloat16 [4, 1024, 1024], P('dp', 'context'), may hold values from -6 to 6
- segments: int32 [4, 1024], P('dp'), may hold values from 0 to 7, as said below
- w_qkv: bfloat16 [1024, 3, 1024], P(('dp', 'context'), None, 'tensor'), may hold values from -0.1875 to 0.1875
- bias_qv: bfloat16 [2, 2, 512], P(None, 'tensor', ('dp', 'context')), may hold values from -1.1953125 to 1.1953125
- w_out: bfloat16 [1024, 1024], P('tensor', ('dp', 'context')), may hold values from -3 to 3
- w_up: bfloat16 [1024, 4096], P(('dp', 'context'), 'tensor'), may hold values from -0.1875 to 0.1875
- bias_up: bfloat16 [2, 2048], P('tensor', ('dp', 'context')), may hold values from -1.1953125 to 1.1953125
- w_down: bfloat16 [4096, 1024], P('tensor', ('dp', 'context')), may hold values from -0.09375 to 0.09375
- norm_gains: bfloat16 [2, 1024], P(None, ('dp', 'context')), may hold values from 0.5 to 1.5
- shifts: bfloat16 [4, 1024], P(None, ('dp', 'context')), may hold values from -1.1953125 to 1.1953125
- cotangent: bfloat16 [4, 1024, 1024], P('dp', 'context'), may hold values from -6 to 6
Outputs:
- layer_output: bfloat16 [4, 1024, 1024], P('dp', 'context')
- grad_input: float32 [4, 1024, 1024], P('dp', 'context')
- grad_w_qkv: float32 [1024, 3, 1024], P(('dp', 'context'), None, 'tensor')
- grad_bias_qv: float32 [2, 2, 512], P(None, 'tensor', ('dp', 'context'))
- grad_w_out: float32 [1024, 1024], P('tensor', ('dp', 'context'))
- grad_w_up: float32 [1024, 4096], P(('dp', 'context'), 'tensor')
- grad_bias_up: float32 [2, 2048], P('tensor', ('dp', 'context'))
- grad_w_down: float32 [4096, 1024], P('tensor', ('dp', 'context'))
- grad_norm_gains: float32 [2, 1024], P(None, ('dp', 'context'))
- grad_shifts: float32 [4, 1024], P(None, ('dp', 'context'))
Inputs may be any that keep to these rules, and one draw needn't show every extreme that they name: `segments`: segment numbers never fall along a row; in every aligned group of 2 rows one row, drawn from the seed, is a single segment.
All inputs are finite; a program needn't handle non-finite values.
Results may differ from a plain program's by a relative error of at most 0.012.
Values may be sent and summed in bfloat16 or wider, within the bound.
A program may use at most 448 MiB of HBM per device.

v0:
```python
from functools import partial
import math

import jax
import jax.numpy as jnp
from jax import lax
from jax.sharding import PartitionSpec as P

HEAD_DIM = 64


def normalize(values):
    center = jnp.mean(values, axis=-1, keepdims=True)
    shifted = values - center
    inverse = lax.rsqrt(jnp.mean(shifted * shifted, axis=-1, keepdims=True) + 1e-05)
    return (shifted * inverse, inverse)


def norm_back(grad, normed, inverse, gain):
    scaled = grad * gain
    return inverse * (
        scaled
        - jnp.mean(scaled, axis=-1, keepdims=True)
        - normed * jnp.mean(scaled * normed, axis=-1, keepdims=True)
    )


def split_heads(block_rows):
    return block_rows.reshape(block_rows.shape[0], -1, HEAD_DIM)


def masked_scores(queries, keys, query_seg, key_seg, query_pos, key_pos):
    scores = jnp.einsum(
        "qhd,khd->hqk", split_heads(queries), split_heads(keys), preferred_element_type=jnp.float32
    ) * (1.0 / math.sqrt(HEAD_DIM))
    mask = (query_pos[:, None] >= key_pos[None, :]) & (query_seg[:, None] == key_seg[None, :])
    return jnp.where(mask[None], scores, -1e30)


def shards(
    layer_input,
    segments,
    w_qkv,
    bias_qv,
    w_out,
    w_up,
    bias_up,
    w_down,
    norm_gains,
    shifts,
    cotangent,
):
    rows, span_len, width = layer_input.shape
    length = segments.shape[1]
    head_scale = 1.0 / math.sqrt(HEAD_DIM)
    begin = lax.axis_index("context") * span_len
    full_qkv, full_bias, full_out, full_up, full_upbias, full_down, gains, offsets = (
        lax.all_gather(w_qkv, ("dp", "context"), axis=0, tiled=True),
        lax.all_gather(bias_qv, ("dp", "context"), axis=2, tiled=True),
        lax.all_gather(w_out, ("dp", "context"), axis=1, tiled=True),
        lax.all_gather(w_up, ("dp", "context"), axis=0, tiled=True),
        lax.all_gather(bias_up, ("dp", "context"), axis=1, tiled=True),
        lax.all_gather(w_down, ("dp", "context"), axis=1, tiled=True),
        lax.all_gather(norm_gains, ("dp", "context"), axis=1, tiled=True),
        lax.all_gather(shifts, ("dp", "context"), axis=1, tiled=True),
    )
    gains = gains.astype(jnp.float32)
    offsets = offsets.astype(jnp.float32)
    query_pos = begin + jnp.arange(span_len, dtype=jnp.int32)
    key_pos = jnp.arange(length, dtype=jnp.int32)
    query_seg = lax.dynamic_slice_in_dim(segments, begin, span_len, 1)
    inputs = layer_input.astype(jnp.float32)
    normed_one, inverse_one = normalize(inputs)
    first = (normed_one * gains[0] + offsets[0]).astype(jnp.bfloat16)
    projected = jnp.einsum("rcd,dkf->rckf", first, full_qkv, preferred_element_type=jnp.float32)
    queries = (projected[:, :, 0] + full_bias[0, 0].astype(jnp.float32)).astype(jnp.bfloat16)
    keys = projected[:, :, 1].astype(jnp.bfloat16)
    values = (projected[:, :, 2] + full_bias[1, 0].astype(jnp.float32)).astype(jnp.bfloat16)
    key_rows, value_rows = (
        lax.all_gather(keys, "context", axis=1, tiled=True),
        lax.all_gather(values, "context", axis=1, tiled=True),
    )

    def forward_row(packed):
        query_row, key_row, value_row, seg_here, seg_all = packed
        scores = masked_scores(query_row, key_row, seg_here, seg_all, query_pos, key_pos)
        top = jnp.max(scores, axis=-1, keepdims=True)
        exponent = jnp.exp(scores - top)
        total = jnp.sum(exponent, axis=-1, keepdims=True)
        weights = exponent / total
        result_row = jnp.einsum(
            "hqk,khd->qhd",
            weights.astype(jnp.bfloat16),
            split_heads(value_row),
            preferred_element_type=jnp.float32,
        )
        return (result_row.reshape(span_len, -1), (top + jnp.log(total))[..., 0])

    mixed, log_totals = lax.map(forward_row, (queries, key_rows, value_rows, query_seg, segments))
    mixed = mixed.astype(jnp.bfloat16)
    branch = (
        lax.psum(
            jnp.einsum("rcf,fd->rcd", mixed, full_out, preferred_element_type=jnp.float32), "tensor"
        )
        + offsets[2]
    )
    hidden = inputs + branch
    normed_two, inverse_two = normalize(hidden)
    second = (normed_two * gains[1] + offsets[1]).astype(jnp.bfloat16)
    upward = jnp.einsum(
        "rcd,df->rcf", second, full_up, preferred_element_type=jnp.float32
    ) + full_upbias[0].astype(jnp.float32)
    active, gelu_back = jax.vjp(partial(jax.nn.gelu, approximate=True), upward)
    active_low = active.astype(jnp.bfloat16)
    down = (
        lax.psum(
            jnp.einsum(
                "rcf,fd->rcd", active_low, full_down, preferred_element_type=jnp.float32
            ).astype(jnp.bfloat16),
            "tensor",
        ).astype(jnp.float32)
        + offsets[3]
    )
    result = (hidden + down).astype(jnp.bfloat16)
    grad_out = cotangent.astype(jnp.float32)
    down_grad = jnp.einsum("rcf,rcd->fd", active_low, cotangent, preferred_element_type=jnp.float32)
    active_grad = jnp.einsum(
        "rcd,fd->rcf", cotangent, full_down, preferred_element_type=jnp.float32
    )
    up_grad = gelu_back(active_grad)[0].astype(jnp.bfloat16)
    upbias_grad = jnp.sum(up_grad, axis=(0, 1), dtype=jnp.float32)[None]
    upw_grad = jnp.einsum("rcd,rcf->df", second, up_grad, preferred_element_type=jnp.float32)
    second_grad = lax.psum(
        jnp.einsum("rcf,df->rcd", up_grad, full_up, preferred_element_type=jnp.float32), "tensor"
    )
    hidden_grad = grad_out + norm_back(second_grad, normed_two, inverse_two, gains[1])
    branch_low = hidden_grad.astype(jnp.bfloat16)
    outw_grad = jnp.einsum("rcf,rcd->fd", mixed, branch_low, preferred_element_type=jnp.float32)
    mixed_grad = jnp.einsum(
        "rcd,fd->rcf", branch_low, full_out, preferred_element_type=jnp.float32
    ).astype(jnp.bfloat16)

    def query_side(packed):
        query_row, key_row, value_row, seg_here, seg_all, grad_row, log_row = packed
        scores = masked_scores(query_row, key_row, seg_here, seg_all, query_pos, key_pos)
        weights = jnp.exp(scores - log_row[..., None])
        weight_grad = jnp.einsum(
            "qhd,khd->hqk",
            split_heads(grad_row),
            split_heads(value_row),
            preferred_element_type=jnp.float32,
        )
        inner = jnp.sum(weights * weight_grad, axis=-1)
        score_grad = (weights * (weight_grad - inner[..., None])).astype(jnp.bfloat16)
        query_grad = (
            jnp.einsum(
                "hqk,khd->qhd", score_grad, split_heads(key_row), preferred_element_type=jnp.float32
            )
            * head_scale
        ).reshape(span_len, -1)
        key_term = (
            jnp.einsum(
                "hqk,qhd->khd",
                score_grad,
                split_heads(query_row),
                preferred_element_type=jnp.float32,
            )
            * head_scale
        )
        value_term = jnp.einsum(
            "hqk,qhd->khd",
            weights.astype(jnp.bfloat16),
            split_heads(grad_row),
            preferred_element_type=jnp.float32,
        )
        return (query_grad, (key_term.reshape(length, -1), value_term.reshape(length, -1)))

    query_grad, extra = lax.map(
        query_side, (queries, key_rows, value_rows, query_seg, segments, mixed_grad, log_totals)
    )
    key_sum, value_sum = lax.psum_scatter(extra, "context", scatter_dimension=1, tiled=True)
    key_grad = key_sum.astype(jnp.bfloat16)
    value_grad = value_sum.astype(jnp.bfloat16)
    query_low = query_grad.astype(jnp.bfloat16)
    stacked_grads = jnp.stack([query_low, key_grad, value_grad], axis=2)
    qkv_grad = jnp.einsum("rcd,rckf->dkf", first, stacked_grads, preferred_element_type=jnp.float32)
    bias_grad = jnp.stack(
        [
            jnp.sum(query_low, axis=(0, 1), dtype=jnp.float32),
            jnp.sum(value_grad, axis=(0, 1), dtype=jnp.float32),
        ]
    )[:, None]
    first_grad = lax.psum(
        jnp.einsum(
            "rckf,dkf->rcd", stacked_grads, full_qkv, preferred_element_type=jnp.float32
        ).astype(jnp.bfloat16),
        "tensor",
    ).astype(jnp.float32)
    input_grad = hidden_grad + norm_back(first_grad, normed_one, inverse_one, gains[0])
    gain_grad = jnp.stack(
        [
            jnp.sum(first_grad * normed_one, axis=(0, 1)),
            jnp.sum(second_grad * normed_two, axis=(0, 1)),
        ]
    )
    offset_grad = jnp.stack(
        [
            jnp.sum(first_grad, axis=(0, 1)),
            jnp.sum(second_grad, axis=(0, 1)),
            jnp.sum(branch_low, axis=(0, 1), dtype=jnp.float32),
            jnp.sum(cotangent, axis=(0, 1), dtype=jnp.float32),
        ]
    )
    sent_qkv, sent_bias, sent_out, sent_up, sent_upbias, sent_down, sent_gain, sent_offset = (
        lax.psum_scatter(qkv_grad, ("dp", "context"), scatter_dimension=0, tiled=True),
        lax.psum_scatter(bias_grad, ("dp", "context"), scatter_dimension=2, tiled=True),
        lax.psum_scatter(outw_grad, ("dp", "context"), scatter_dimension=1, tiled=True),
        lax.psum_scatter(upw_grad, ("dp", "context"), scatter_dimension=0, tiled=True),
        lax.psum_scatter(upbias_grad, ("dp", "context"), scatter_dimension=1, tiled=True),
        lax.psum_scatter(down_grad, ("dp", "context"), scatter_dimension=1, tiled=True),
        lax.psum_scatter(gain_grad, ("dp", "context"), scatter_dimension=1, tiled=True),
        lax.psum_scatter(offset_grad, ("dp", "context"), scatter_dimension=1, tiled=True),
    )
    return (
        result,
        input_grad,
        sent_qkv,
        sent_bias,
        sent_out,
        sent_up,
        sent_upbias,
        sent_down,
        sent_gain,
        sent_offset,
    )


def solution(mesh):
    return jax.shard_map(
        shards,
        mesh=mesh,
        in_specs=(
            P("dp", "context", None),
            P("dp", None),
            P(("dp", "context"), None, "tensor"),
            P(None, "tensor", ("dp", "context")),
            P("tensor", ("dp", "context")),
            P(("dp", "context"), "tensor"),
            P("tensor", ("dp", "context")),
            P("tensor", ("dp", "context")),
            P(None, ("dp", "context")),
            P(None, ("dp", "context")),
            P("dp", "context", None),
        ),
        out_specs=(
            P("dp", "context", None),
            P("dp", "context", None),
            P(("dp", "context"), None, "tensor"),
            P(None, "tensor", ("dp", "context")),
            P("tensor", ("dp", "context")),
            P(("dp", "context"), "tensor"),
            P("tensor", ("dp", "context")),
            P("tensor", ("dp", "context")),
            P(None, ("dp", "context")),
            P(None, ("dp", "context")),
        ),
        check_vma=False,
    )
```

profile of v0, /device:TPU:0, one launch (start us, length us, event | category | flops | bytes accessed | tf_op | source)
XLA Modules:
  0.0 1322.9 jit_solution(8059641476399215459)
XLA Ops:
  8.0 34.4 %all-gather.2 = bf16[16,64,4]{1,2,0:T(4,128)(2,1)S(1)} all-gather(bf16[1,64,4]{1,2,0:T(4,128)(2,1)} %bitcast.271), channel_id=1, replica_groups=mesh['dp'=2,'context'=8,'tensor'=2] {'dp','context'}, dimensions={0}, use_global_device_ids=true | all-gather | bytes 8704 | tf_op jit(solution)/shard_map/all_gather | solution.py:65
  42.4 28.5 %all-gather.1 = bf16[16,64,2]{1,2,0:T(2,128)(2,1)S(1)} all-gather(bf16[1,64,2]{1,2,0:T(2,128)(2,1)} %bitcast.272), channel_id=1, replica_groups=mesh['dp'=2,'context'=8,'tensor'=2] {'dp','context'}, dimensions={0}, use_global_device_ids=true | all-gather | bytes 4352 | tf_op jit(solution)/shard_map/all_gather | solution.py:64
  74.2 3.2 fusion.36
  78.3 33.8 %all_gather.33 = bf16[2,1,512]{1,0,2:T(2,128)(2,1)S(1)} all-gather(bf16[2,1,32]{1,0,2:T(2,128)(2,1)S(1)} %copy.99), channel_id=1, replica_groups=mesh['dp'=2,'context'=8,'tensor'=2] {'dp','context'}, dimensions={2}, use_global_device_ids=true | all-gather | bytes 2176 | tf_op jit(solution)/shard_map/all_gather | solution.py:59
  116.7 11.2 all-gather.20.cloned.1.call-done
  127.9 4.0 copy.102
  131.9 46.7 %all-gather.12.cloned.1.call-done = bf16[2,1024,512]{2,1,0:T(8,128)(2,1)} async-done(((bf16[2,128,512]{2,1,0:T(8,128)(2,1)}), bf16[2,1024,512]{2,1,0:T(8,128)(2,1)}) %all-gather.12.cloned.1.call-update) | async-done | bytes 2097168 | tf_op jit(solution)/shard_map/all_gather | solution.py:81
  178.7 4.0 copy.100
  182.7 12.8 while.28
  195.5 21.7 %all-gather.14.cloned.1.call-done = bf16[512,1024]{0,1:T(8,128)(2,1)} async-done(((bf16[512,64]{0,1:T(8,128)(2,1)}), bf16[512,1024]{0,1:T(8,128)(2,1)}) %all-gather.14.cloned.1.call-update) | async-done | bytes 1048592 | tf_op jit(solution)/shard_map/all_gather | solution.py:60
  217.2 2.7 fusion.75
  221.3 30.5 %all_gather.38 = bf16[1,2048]{1,0:T(2,128)(2,1)S(1)} all-gather(bf16[1,128]{1,0:T(2,128)(2,1)S(1)} %copy-done.48), channel_id=1, replica_groups=mesh['dp'=2,'context'=8,'tensor'=2] {'dp','context'}, dimensions={1}, use_global_device_ids=true | all-gather | bytes 4352 | tf_op jit(solution)/shard_map/all_gather | solution.py:62
  251.8 7.3 all-reduce.5.cloned.1.call-done
  260.8 51.1 %all-gather.16.cloned.1.call-done = bf16[1024,2048]{1,0:T(8,128)(2,1)} async-done(((bf16[64,2048]{1,0:T(8,128)(2,1)}), bf16[1024,2048]{1,0:T(8,128)(2,1)}) %all-gather.16.cloned.1.call-update) | async-done | bytes 4194320 | tf_op jit(solution)/shard_map/all_gather | solution.py:61
  311.9 3.5 fusion.38
  315.5 48.0 %all-gather.18.cloned.1.call-done = bf16[2048,1024]{0,1:T(8,128)(2,1)} async-done(((bf16[2048,64]{0,1:T(8,128)(2,1)}), bf16[2048,1024]{0,1:T(8,128)(2,1)}) %all-gather.18.cloned.1.call-update) | async-done | bytes 4194320 | tf_op jit(solution)/shard_map/all_gather | solution.py:63
  363.5 5.4 convert_reduce_fusion
  372.3 38.6 %all-reduce.7.cloned.1.call-done = f32[2,128,1024]{2,1,0:T(8,128)} async-done(((f32[2,128,1024]{2,1,0:T(8,128)}), f32[2,128,1024]{2,1,0:T(8,128)}) %all-reduce.7.cloned.1.call-update) | async-done | bytes 1048592 | tf_op jit(solution)/shard_map/psum | solution.py:133
  410.9 2.4 multiply_reduce_fusion.1
  416.6 65.3 %while.29 = (s32[]{:T(128)}, bf16[2,128,512]{2,1,0:T(8,128)(2,1)}, f32[2,1024,512]{2,1,0:T(8,128)}, f32[2,1024,512]{2,1,0:T(8,128)}, bf16[2,1024,512]{1,2,0:T(8,...) while((s32[]{:T(128)}, bf16[2,128,512]{2,1,0:T(8,128)(2,1)}, ...), condition=%wide.region_15.16_spmd.clone, body=%wide.region_13.15_spmd.clone.sunk | while | flops 687864960 | bytes 87542616 | solution.py:178
  418.9 2.7 fusion.154
  424.1 4.1 multiply_reduce_fusion.6
  432.7 4.8 fusion.157
  437.4 2.9 copy.167
  442.1 3.1 copy.168
  445.2 4.1 constant_dynamic-update-slice_fusion.9
  451.5 2.7 fusion.154
  456.8 4.1 multiply_reduce_fusion.6
  465.4 4.8 fusion.157
  470.1 2.9 copy.167
  474.8 3.1 copy.168
  477.8 4.0 constant_dynamic-update-slice_fusion.9
  483.6 4.5 fusion.59
  488.0 82.0 %reduce-scatter.21.cloned.1.call-done = f32[2,128,512]{2,1,0:T(8,128)} async-done(((f32[2,1024,512]{2,1,0:T(8,128)}), f32[2,128,512]{2,1,0:T(8,128)}) %reduce-scatter.21.cloned.1.call-update) | async-done | bytes 524304 | tf_op jit(solution)/shard_map/reduce_scatter | solution.py:181
  571.1 90.5 %reduce-scatter.19.cloned.1.call-done = f32[2,128,512]{2,1,0:T(8,128)} async-done(((f32[2,1024,512]{2,1,0:T(8,128)}), f32[2,128,512]{2,1,0:T(8,128)}) %reduce-scatter.19.cloned.1.call-update) | async-done | bytes 524304 | tf_op jit(solution)/shard_map/reduce_scatter | solution.py:181
  663.4 3.7 fusion.56
  670.5 36.7 %all-reduce.9.cloned.1.call-done = (bf16[2,128,1024]{2,1,0:T(8,128)(2,1)}, bf16[2,128,1024]{2,1,0:T(8,128)(2,1)}) async-done(((bf16[2,128,1024]{2,1,0:T(8,128)(2,1)}, bf16[2,128,1024]{2,1,0:T(8,128)(2,1)}), (bf16[2,128,1024]{2,1,0:T(8,128)(2,1)}, bf16[2,128,1024]{2,1,0:T(8,128)(2,1)})) %all-reduce.9.cloned.1.call-update) | async-done | bytes 1048592 | tf_op jit(solution)/shard_map/psum | solution.py:116
  713.4 5.9 convolution_bitcast_fusion.1
  720.3 6.3 convolution_bitcast_fusion
  727.7 3.8 convolution_bitcast_fusion.2
  731.5 37.1 %reduce-scatter.33.cloned.1.call-done = f32[128,1]{1,0:T(8,128)} async-done(((f32[2048,1]{1,0:T(8,128)}), f32[128,1]{1,0:T(8,128)}) %reduce-scatter.33.cloned.1.call-update) | async-done | bytes 528
  770.0 56.4 %reduce-scatter.31.cloned.1.call-done = f32[32,2]{1,0:T(8,128)} async-done(((f32[512,2]{1,0:T(8,128)}), f32[32,2]{1,0:T(8,128)}) %reduce-scatter.31.cloned.1.call-update) | async-done | bytes 272
  831.3 53.4 %reduce-scatter.35.cloned.1.call-done = f32[64,2]{1,0:T(8,128)} async-done(((f32[1024,2]{1,0:T(8,128)}), f32[64,2]{1,0:T(8,128)}) %reduce-scatter.35.cloned.1.call-update) | async-done | bytes 528
  886.1 57.2 %reduce-scatter.37.cloned.1.call-done = f32[64,4]{1,0:T(8,128)} async-done(((f32[1024,4]{1,0:T(8,128)}), f32[64,4]{1,0:T(8,128)}) %reduce-scatter.37.cloned.1.call-update) | async-done | bytes 1040
  944.7 63.4 %reduce-scatter.25.cloned.1.call-done = f32[512,64]{0,1:T(8,128)} async-done(((f32[512,1024]{0,1:T(8,128)}), f32[512,64]{0,1:T(8,128)}) %reduce-scatter.25.cloned.1.call-update) | async-done | bytes 131088 | tf_op jit(solution)/shard_map/reduce_scatter | solution.py:217
  1008.1 108.8 %reduce-scatter.27.cloned.1.call-done = f32[64,2048]{1,0:T(8,128)} async-done(((f32[1024,2048]{1,0:T(8,128)}), f32[64,2048]{1,0:T(8,128)}) %reduce-scatter.27.cloned.1.call-update) | async-done | bytes 524304 | tf_op jit(solution)/shard_map/reduce_scatter | solution.py:218
  1116.9 109.5 %reduce-scatter.29.cloned.1.call-done = f32[2048,64]{0,1:T(8,128)} async-done(((f32[2048,1024]{0,1:T(8,128)}), f32[2048,64]{0,1:T(8,128)}) %reduce-scatter.29.cloned.1.call-update) | async-done | bytes 524304 | tf_op jit(solution)/shard_map/reduce_scatter | solution.py:220
  1226.3 90.1 %reduce-scatter.23.cloned.1.call-done = f32[64,3,512]{2,0,1:T(8,128)} async-done(((f32[1024,3,512]{2,0,1:T(8,128)}), f32[64,3,512]{2,0,1:T(8,128)}) %reduce-scatter.23.cloned.1.call-update) | async-done | bytes 393232 | tf_op jit(solution)/shard_map/reduce_scatter | solution.py:215
  (256 shorter events, 78.9 us)
Async XLA Ops:
  7.2 67.0 %all-gather.10.cloned.1.call-start = ((), (), s32[]{:S(2)}) async-start(), calls=%async_computation.10 | async-start | bytes 3342336 | tf_op jit(solution)/shard_map/all_gather | solution.py:58
  7.9 120.0 %all-gather.20.cloned.1.call-start = ((), (), s32[]{:S(2)}) async-start(), calls=%async_computation.23 | async-start | bytes 2359296 | tf_op jit(solution)/shard_map/all_gather | solution.py:80
  72.2 5.2 copy-start.38
  74.2 237.8 %copy-start.23 = (f32[1,1024]{1,0:T(1,128)}, f32[1,1024]{1,0:T(1,128)S(1)}, u32[]{:S(2)}) copy-start(f32[1,1024]{1,0:T(1,128)S(1)} %get-tuple-element.364) | copy-start | bytes 12292
  77.4 38.5 %copy-start.22 = (s32[2,1024]{1,0:T(2,128)S(1)}, s32[2,1024]{1,0:T(2,128)}, u32[]{:S(2)}) copy-start(s32[2,1024]{1,0:T(2,128)} %param.16) | copy-start | bytes 24580
  78.2 100.5 %all-gather.12.cloned.1.call-start = ((), (), s32[]{:S(2)}) async-start(), calls=%async_computation.11 | async-start | bytes 2359296 | tf_op jit(solution)/shard_map/all_gather | solution.py:81
  115.2 102.0 %all-gather.14.cloned.1.call-start = ((), (), s32[]{:S(2)}) async-start(), calls=%async_computation.12 | async-start | bytes 1114112 | tf_op jit(solution)/shard_map/all_gather | solution.py:60
  115.8 143.3 %all-reduce.5.cloned.1.call-start = ((), (), s32[]{:S(2)}) async-start(), calls=%async_computation.13 | async-start | bytes 2097152 | tf_op jit(solution)/shard_map/psum | solution.py:102
  195.5 63.6 %copy-start.16 = (bf16[2,128,512]{1,2,0:T(8,128)(2,1)}, bf16[2,128,512]{1,2,0:T(8,128)(2,1)S(1)}, u32[]{:S(2)}) copy-start(bf16[2,128,512]{1,2,0:T(8,128)(2,1)S(1)} %get-tuple-element.132) | copy-start | bytes 786436
  195.5 25.8 %copy-start.48 = (bf16[1,128]{1,0:T(2,128)(2,1)S(1)}, bf16[1,128]{1,0:T(2,128)(2,1)}, u32[]{:S(2)}) copy-start(bf16[1,128]{1,0:T(2,128)(2,1)} %param.21) | copy-start | bytes 772
  195.5 63.6 %copy-start.6 = (bf16[2,128,1024]{2,1,0:T(8,128)(2,1)S(1)}, bf16[2,128,1024]{2,1,0:T(8,128)(2,1)}, u32[]{:S(2)}) copy-start(bf16[2,128,1024]{2,1,0:T(8,128)(2,1)} %param.15) | copy-start | bytes 1572868
  219.9 92.0 %all-gather.16.cloned.1.call-start = ((), (), s32[]{:S(2)}) async-start(), calls=%async_computation.14 | async-start | bytes 4456448 | tf_op jit(solution)/shard_map/all_gather | solution.py:61
  220.5 142.9 %all-gather.18.cloned.1.call-start = ((), (), s32[]{:S(2)}) async-start(), calls=%async_computation.15 | async-start | bytes 4456448 | tf_op jit(solution)/shard_map/all_gather | solution.py:63
  221.3 189.7 %all-reduce.7.cloned.1.call-start = ((), (), s32[]{:S(2)}) async-start(), calls=%async_computation.16 | async-start | bytes 2097152 | tf_op jit(solution)/shard_map/psum | solution.py:133
  260.5 152.8 %copy-start.2 = (f32[2,128,1024]{2,1,0:T(8,128)}, f32[2,128,1024]{2,1,0:T(8,128)S(1)}, u32[]{:S(2)}) copy-start(f32[2,128,1024]{2,1,0:T(8,128)S(1)} %get-tuple-element.349) | copy-start | bytes 3145732
  260.5 152.8 %copy-start.29 = (f32[2,128]{1,0:T(2,128)}, f32[2,128]{1,0:T(2,128)S(1)}, u32[]{:S(2)}) copy-start(f32[2,128]{1,0:T(2,128)S(1)} %broadcast_multiply_fusion.4) | copy-start | bytes 3076
  260.8 152.5 %copy-start.31 = (f32[2,128]{1,0:T(2,128)}, f32[2,128]{1,0:T(2,128)S(1)}, u32[]{:S(2)}) copy-start(f32[2,128]{1,0:T(2,128)S(1)} %add_rsqrt_fusion) | copy-start | bytes 3076
  315.5 53.4 %copy-start.10 = (f32[2,128,2048]{2,1,0:T(8,128)}, f32[2,128,2048]{2,1,0:T(8,128)S(1)}, u32[]{:S(2)}) copy-start(f32[2,128,2048]{2,1,0:T(8,128)S(1)} %fusion.38) | copy-start | bytes 6291460
  363.5 6.4 copy-start.49
  372.2 41.2 %copy-start.12 = (bf16[2,128,1024]{2,1,0:T(8,128)(2,1)S(1)}, bf16[2,128,1024]{2,1,0:T(8,128)(2,1)}, u32[]{:S(2)}) copy-start(bf16[2,128,1024]{2,1,0:T(8,128)(2,1)} %param.25) | copy-start | bytes 1572868
  372.2 197.8 %reduce-scatter.21.cloned.1.call-start = ((), (), s32[]{:S(2)}) async-start(), calls=%async_computation.18 | async-start | bytes 4718592 | tf_op jit(solution)/shard_map/reduce_scatter | solution.py:181
  416.6 4.9 copy-start.25
  416.6 4.9 copy-start.45
  449.3 4.9 copy-start.25
  449.3 4.9 copy-start.45
  481.9 179.7 %reduce-scatter.19.cloned.1.call-start = ((), (), s32[]{:S(2)}) async-start(), calls=%async_computation.17 | async-start | bytes 4718592 | tf_op jit(solution)/shard_map/reduce_scatter | solution.py:181
  482.5 180.9 %copy-start.20 = (bf16[2,128,512]{2,1,0:T(8,128)(2,1)S(1)}, bf16[2,128,512]{2,1,0:T(8,128)(2,1)}, u32[]{:S(2)}) copy-start(bf16[2,128,512]{2,1,0:T(8,128)(2,1)} %get-tuple-element.134) | copy-start | bytes 786436
  482.5 224.7 %all-reduce.9.cloned.1.call-start = ((), (), s32[]{:S(2)}) async-start(), calls=%async_computation.28 | async-start | bytes 2097152 | tf_op jit(solution)/shard_map/psum | solution.py:116
  667.1 40.1 %copy-start.7 = (bf16[2,128,1024]{2,1,0:T(8,128)(2,1)S(1)}, bf16[2,128,1024]{2,1,0:T(8,128)(2,1)}, u32[]{:S(2)}) copy-start(bf16[2,128,1024]{2,1,0:T(8,128)(2,1)} %param.15) | copy-start | bytes 1572868
  667.1 40.1 %copy-start.28 = (f32[1,1024]{1,0:T(1,128)S(1)}, f32[1,1024]{1,0:T(1,128)}, u32[]{:S(2)}) copy-start(f32[1,1024]{1,0:T(1,128)} %copy-done.27) | copy-start | bytes 12292
  667.1 40.1 %copy-start.39 = (f32[2,128]{1,0:T(2,128)S(1)}, f32[2,128]{1,0:T(2,128)}, u32[]{:S(2)}) copy-start(f32[2,128]{1,0:T(2,128)} %copy-done.38) | copy-start | bytes 3076
  667.1 40.1 %copy-start.41 = (f32[2,128]{1,0:T(2,128)S(1)}, f32[2,128]{1,0:T(2,128)}, u32[]{:S(2)}) copy-start(f32[2,128]{1,0:T(2,128)} %copy-done.40) | copy-start | bytes 3076
  667.1 101.4 %reduce-scatter.33.cloned.1.call-start = ((), (), s32[]{:S(2)}) async-start(), calls=%async_computation.25 | async-start | bytes 1114112
  668.6 40.2 %copy-start.33 = (f32[1024]{0:T(1024)S(1)}, f32[1024]{0:T(1024)}, u32[]{:S(2)}) copy-start(f32[1024]{0:T(1024)} %get-tuple-element.292) | copy-start | bytes 12292
  668.7 41.3 %copy-start.35 = (f32[1024]{0:T(1024)S(1)}, f32[1024]{0:T(1024)}, u32[]{:S(2)}) copy-start(f32[1024]{0:T(1024)} %get-tuple-element.297) | copy-start | bytes 12292
  668.7 41.3 %copy-start.36 = (f32[1024]{0:T(1024)S(1)}, f32[1024]{0:T(1024)}, u32[]{:S(2)}) copy-start(f32[1024]{0:T(1024)} %get-tuple-element.346) | copy-start | bytes 12292
  668.7 41.3 %copy-start.37 = (f32[1024]{0:T(1024)S(1)}, f32[1024]{0:T(1024)}, u32[]{:S(2)}) copy-start(f32[1024]{0:T(1024)} %get-tuple-element.360) | copy-start | bytes 12292
  668.7 157.7 %reduce-scatter.31.cloned.1.call-start = ((), (), s32[]{:S(2)}) async-start(), calls=%async_computation.24 | async-start | bytes 278528
  669.1 42.3 %copy-start.5 = (f32[2,128,1024]{2,1,0:T(8,128)S(1)}, f32[2,128,1024]{2,1,0:T(8,128)}, u32[]{:S(2)}) copy-start(f32[2,128,1024]{2,1,0:T(8,128)} %copy-done.4) | copy-start | bytes 3145732
  669.1 42.3 %copy-start.17 = (bf16[2,128,512]{1,2,0:T(8,128)(2,1)S(1)}, bf16[2,128,512]{1,2,0:T(8,128)(2,1)}, u32[]{:S(2)}) copy-start(bf16[2,128,512]{1,2,0:T(8,128)(2,1)} %copy-done.16) | copy-start | bytes 786436
  670.5 214.2 %reduce-scatter.35.cloned.1.call-start = ((), (), s32[]{:S(2)}) async-start(), calls=%async_computation.26 | async-start | bytes 557056
  710.0 233.4 %reduce-scatter.37.cloned.1.call-start = ((), (), s32[]{:S(2)}) async-start(), calls=%async_computation.27 | async-start | bytes 557056
  711.2 296.9 %reduce-scatter.25.cloned.1.call-start = ((), (), s32[]{:S(2)}) async-start(), calls=%async_computation.20 | async-start | bytes 2228224 | tf_op jit(solution)/shard_map/reduce_scatter | solution.py:217
  713.3 403.5 %reduce-scatter.27.cloned.1.call-start = ((), (), s32[]{:S(2)}) async-start(), calls=%async_computation.21 | async-start | bytes 8912896 | tf_op jit(solution)/shard_map/reduce_scatter | solution.py:218
  719.3 507.0 %reduce-scatter.29.cloned.1.call-start = ((), (), s32[]{:S(2)}) async-start(), calls=%async_computation.22 | async-start | bytes 8912896 | tf_op jit(solution)/shard_map/reduce_scatter | solution.py:220
  726.7 589.7 %reduce-scatter.23.cloned.1.call-start = ((), (), s32[]{:S(2)}) async-start(), calls=%async_computation.19 | async-start | bytes 6684672 | tf_op jit(solution)/shard_map/reduce_scatter | solution.py:215
  731.5 96.4 %copy-start.34 = (f32[1,1024]{1,0:T(1,128)S(1)}, f32[1,1024]{1,0:T(1,128)}, u32[]{:S(2)}) copy-start(f32[1,1024]{1,0:T(1,128)} %get-tuple-element.363) | copy-start | bytes 12292
  731.5 98.4 %copy-start.14 = (bf16[2,128,1024]{2,1,0:T(8,128)(2,1)S(1)}, bf16[2,128,1024]{2,1,0:T(8,128)(2,1)}, u32[]{:S(2)}) copy-start(bf16[2,128,1024]{2,1,0:T(8,128)(2,1)} %get-tuple-element.345) | copy-start | bytes 1572868
  (27 other events, 71.5 us)
Sparse Core Ops, SparseCore 0:
  10.2 48.1 all-gather.9
  78.3 49.6 all-gather.19
  130.7 47.8 all-gather.11
  180.7 36.4 all-gather.13
  220.0 38.9 all-reduce.4
  261.3 50.5 all-gather.15
  314.4 49.0 all-gather.17
  372.3 38.5 all-reduce.6
  482.0 87.8 reduce-scatter.20
  573.9 87.6 reduce-scatter.18
  667.2 39.9 all-reduce.8
  711.1 57.3 reduce-scatter.32
  772.1 54.2 reduce-scatter.30
  829.8 54.7 reduce-scatter.34
  888.5 54.7 reduce-scatter.36
  947.5 60.5 reduce-scatter.24
  1013.1 103.6 reduce-scatter.26
  1121.9 104.4 reduce-scatter.28
  1231.4 84.9 reduce-scatter.22
where the time goes:
time: 1320 us
  waiting for transfers between devices  1010 us (77%)
  blocking collectives  127 us (10%)
  matrix products  78.5 us (6%)
  local copies, waits for them, and re-layouts  65 us (5%)
  other arithmetic  23.6 us (2%)
  between operations  14.6 us (1%)
    unnamed x23, waiting for transfers between devices  207 us
    reduce_scatter x2, waiting for transfers between devices, shards(): lax.psum_scatter(extra, 'context', scatter_dimension=1, tiled=True)  172 us
    reduce_scatter x1, waiting for transfers between devices, shards(): lax.psum_scatter(down_grad, ('dp', 'context'), scatter_dimension=1, tiled...  109 us
    reduce_scatter x1, waiting for transfers between devices, shards(): lax.psum_scatter(upw_grad, ('dp', 'context'), scatter_dimension=0, tiled=...  109 us
    reduce_scatter x1, waiting for transfers between devices, shards(): lax.psum_scatter(qkv_grad, ('dp', 'context'), scatter_dimension=0, tiled=...  90.1 us
    reduce_scatter x1, waiting for transfers between devices, shards(): lax.psum_scatter(outw_grad, ('dp', 'context'), scatter_dimension=1, tiled...  63.4 us
    all_gather x1, waiting for transfers between devices, shards(): lax.all_gather(w_up, ('dp', 'context'), axis=0, tiled=True)  51.1 us
    all_gather x1, waiting for transfers between devices, shards(): lax.all_gather(w_down, ('dp', 'context'), axis=1, tiled=True)  48 us
  transfers between devices with their start and end apart: 19, of which 18 were waited for; matrix products, arithmetic and copies ran while one was open for 5% of the time, Pallas kernels for 0%

commit v1 on v0

--- a/solution.py
+++ b/solution.py
@@ -4,6 +4,8 @@
 import jax
 import jax.numpy as jnp
 from jax import lax
+from jax.experimental import pallas as pl
+from jax.experimental.pallas import tpu as pltpu
 from jax.sharding import PartitionSpec as P
 
 HEAD_DIM = 64
@@ -37,7 +39,7 @@
     return jnp.where(mask[None], scores, -1e30)
 
 
-def shards(
+def general_shards(
     layer_input,
     segments,
     w_qkv,
@@ -233,6 +235,446 @@
         sent_gain,
         sent_offset,
     )
+
+
+MESH = pl.DeviceIdType.MESH
+VMEM_BYTES = 56 * 1024 * 1024
+
+
+def other_z(z, step, count):
+    if count == 4:
+        return (z + 1 - 2 * (z % 2), (z + 2) % 4, 3 - z)[step - 1]
+    return (z + step) % count
+
+
+def place():
+    d = lax.axis_index("dp")
+    c = lax.axis_index("context")
+    t = lax.axis_index("tensor")
+    return d, c // 2, c % 2, t
+
+
+def greet(peers):
+    barrier = pltpu.get_barrier_semaphore()
+    for peer in peers:
+        pl.semaphore_signal(barrier, inc=1, device_id=peer, device_id_type=MESH)
+    pl.semaphore_wait(barrier, len(peers))
+
+
+def gather_kernel(arrays, nz, *refs):
+    sources, results = refs[:arrays], refs[arrays : 2 * arrays]
+    own_sem, send_sem, recv_sem = refs[2 * arrays :]
+    d, z, x, t = place()
+    nc = 2 * nz
+    here = z * 2 + x
+    peer_x = (d, z * 2 + 1 - x, t)
+    peer_d = (1 - d, here, t)
+    peers_z = [(d, other_z(z, k, nz) * 2 + x, t) for k in range(1, nz)]
+    greet(peers_z + [peer_x, peer_d])
+    pending = []
+
+    def send(a, source, shard, slot, peer):
+        copy = pltpu.make_async_remote_copy(
+            src_ref=source,
+            dst_ref=results[a].at[shard],
+            send_sem=send_sem.at[a, slot],
+            recv_sem=recv_sem.at[a, shard],
+            device_id=peer,
+            device_id_type=MESH,
+        )
+        copy.start()
+        pending.append(copy)
+
+    def arrived(a, shard):
+        pltpu.make_async_remote_copy(
+            src_ref=sources[a],
+            dst_ref=results[a].at[shard],
+            send_sem=send_sem.at[a, 0],
+            recv_sem=recv_sem.at[a, shard],
+            device_id=peer_d,
+            device_id_type=MESH,
+        ).wait_recv()
+
+    mine = d * nc + here
+    locals_ = []
+    for a in range(arrays):
+        for k in range(1, nz):
+            send(a, sources[a], mine, k - 1, peers_z[k - 1])
+        send(a, sources[a], mine, nz - 1, peer_x)
+        send(a, sources[a], mine, 2 * nz - 1, peer_d)
+        keep = pltpu.make_async_copy(sources[a], results[a].at[mine], own_sem.at[a])
+        keep.start()
+        locals_.append(keep)
+    for a in range(arrays):
+        for k in range(nz):
+            row = z if k == 0 else other_z(z, k, nz)
+            if k:
+                shard = d * nc + row * 2 + x
+                arrived(a, shard)
+                send(a, results[a].at[shard], shard, nz - 1 + k, peer_x)
+                send(a, results[a].at[shard], shard, 2 * nz - 1 + k, peer_d)
+            shard = d * nc + row * 2 + 1 - x
+            arrived(a, shard)
+            send(a, results[a].at[shard], shard, 3 * nz - 1 + k, peer_d)
+    for a in range(arrays):
+        for k in range(nc):
+            arrived(a, (1 - d) * nc + k)
+        locals_[a].wait()
+    for copy in pending:
+        copy.wait_send()
+
+
+def gather_weights(nc, *arrays):
+    count = len(arrays)
+    hbm = pl.BlockSpec(memory_space=pl.ANY)
+    results = pl.pallas_call(
+        partial(gather_kernel, count, nc // 2),
+        out_shape=[jax.ShapeDtypeStruct((2 * nc,) + a.shape, a.dtype) for a in arrays],
+        in_specs=[hbm] * count,
+        out_specs=[hbm] * count,
+        scratch_shapes=[
+            pltpu.SemaphoreType.DMA((count,)),
+            pltpu.SemaphoreType.DMA((count, 2 * nc - 1)),
+            pltpu.SemaphoreType.DMA((count, 2 * nc)),
+        ],
+        compiler_params=pltpu.CompilerParams(collective_id=0, has_side_effects=True),
+    )(*arrays)
+    return [r.reshape((-1,) + r.shape[2:]) for r in results]
+
+
+def exchange_kernel(nc, source, result, own_sem, send_sem, recv_sem):
+    d, z, x, t = place()
+    here = z * 2 + x
+    greet([(d, (here + k) % nc, t) for k in range(1, nc)])
+    keep = pltpu.make_async_copy(source.at[here], result.at[here], own_sem)
+    keep.start()
+    copies = []
+    for k in range(1, nc):
+        target = (here + k) % nc
+        copy = pltpu.make_async_remote_copy(
+            src_ref=source.at[target],
+            dst_ref=result.at[here],
+            send_sem=send_sem.at[k],
+            recv_sem=recv_sem.at[k],
+            device_id=(d, target, t),
+            device_id_type=MESH,
+        )
+        copy.start()
+        copies.append(copy)
+    keep.wait()
+    for k, copy in enumerate(copies, 1):
+        copy.wait_send()
+        pltpu.make_async_remote_copy(
+            src_ref=source.at[here],
+            dst_ref=result.at[(here + nc - k) % nc],
+            send_sem=send_sem.at[k],
+            recv_sem=recv_sem.at[k],
+            device_id=(d, (here + k) % nc, t),
+            device_id_type=MESH,
+        ).wait_recv()
+
+
+def exchange(blocks, which):
+    nc = blocks.shape[0]
+    hbm = pl.BlockSpec(memory_space=pl.ANY)
+    return pl.pallas_call(
+        partial(exchange_kernel, nc),
+        out_shape=jax.ShapeDtypeStruct(blocks.shape, blocks.dtype),
+        in_specs=[hbm],
+        out_specs=hbm,
+        scratch_shapes=[
+            pltpu.SemaphoreType.DMA,
+            pltpu.SemaphoreType.DMA((nc,)),
+            pltpu.SemaphoreType.DMA((nc,)),
+        ],
+        compiler_params=pltpu.CompilerParams(collective_id=which, has_side_effects=True),
+    )(blocks)
+
+
+def scatter_kernel(arrays, nz, *refs):
+    grads, results = refs[:arrays], refs[arrays : 2 * arrays]
+    scratch = refs[2 * arrays :]
+    from_d, to_x, from_x, to_z, from_z = (scratch[i * arrays : (i + 1) * arrays] for i in range(5))
+    send_sem, recv_sem = scratch[5 * arrays :]
+    d, z, x, t = place()
+    nc = 2 * nz
+    here = z * 2 + x
+    peer_x = (d, z * 2 + 1 - x, t)
+    peer_d = (1 - d, here, t)
+    rows = [z if k == 0 else other_z(z, k, nz) for k in range(nz)]
+    peers_z = [(d, rows[k] * 2 + x, t) for k in range(1, nz)]
+    greet(peers_z + [peer_x, peer_d])
+    pending = []
+
+    def send(a, source, target, slot, peer):
+        copy = pltpu.make_async_remote_copy(
+            src_ref=source,
+            dst_ref=target,
+            send_sem=send_sem.at[a, slot],
+            recv_sem=recv_sem.at[a, slot],
+            device_id=peer,
+            device_id_type=MESH,
+        )
+        copy.start()
+        pending.append(copy)
+        return copy
+
+    def added(target, *terms):
+        step = 16
+
+        @pl.loop(0, target.shape[0] // step)
+        def _(i):
+            part = pl.ds(pl.multiple_of(i * step, step), step)
+            total = terms[0][part].astype(jnp.float32)
+            for term in terms[1:]:
+                total = total + term[part].astype(jnp.float32)
+            target[part] = total.astype(target.dtype)
+
+    order = list(range(1, nz)) + [0]
+    halves = [[], []]
+    for a in range(arrays):
+        first = {}
+        for side in range(2):
+            for k in order:
+                column = 1 - x if side == 0 else x
+                shard = rows[k] * 2 + column
+                slot = side * nz + k
+                first[slot] = send(
+                    a, grads[a].at[(1 - d) * nc + shard], from_d[a].at[slot], slot, peer_d
+                )
+        halves[0].append(first)
+    for a in range(arrays):
+        second = {}
+        for k in order:
+            halves[0][a][k].wait_recv()
+            added(
+                to_x[a].at[k], grads[a].at[d * nc + rows[k] * 2 + 1 - x], from_d[a].at[k]
+            )
+            second[k] = send(a, to_x[a].at[k], from_x[a].at[k], nc + k, peer_x)
+        halves[1].append(second)
+    last = []
+    for a in range(arrays):
+        third = []
+        for k in order:
+            halves[0][a][nz + k].wait_recv()
+            halves[1][a][k].wait_recv()
+            if k:
+                added(
+                    to_z[a].at[k - 1],
+                    grads[a].at[d * nc + rows[k] * 2 + x],
+                    from_d[a].at[nz + k],
+                    from_x[a].at[k],
+                )
+                back = (nz - k) if nz != 4 else k
+                third.append(
+                    send(a, to_z[a].at[k - 1], from_z[a].at[back - 1], nc + nz + k - 1, peers_z[k - 1])
+                )
+        last.append(third)
+    for a in range(arrays):
+        for copy in last[a]:
+            copy.wait_recv()
+        added(
+            results[a],
+            grads[a].at[d * nc + here],
+            from_d[a].at[nz],
+            from_x[a].at[0],
+            *[from_z[a].at[k] for k in range(nz - 1)],
+        )
+    for copy in pending:
+        copy.wait_send()
+
+
+def scatter_grads(nc, *arrays):
+    count = len(arrays)
+    nz = nc // 2
+    blocks = [a.reshape((2 * nc, -1, a.shape[-1])) for a in arrays]
+    shapes = [b.shape[1:] for b in blocks]
+    vmem = pl.BlockSpec(memory_space=pltpu.VMEM)
+
+    def buffers(number):
+        return [pltpu.VMEM((number,) + s, jnp.bfloat16) for s in shapes]
+
+    return pl.pallas_call(
+        partial(scatter_kernel, count, nz),
+        out_shape=[jax.ShapeDtypeStruct(s, jnp.float32) for s in shapes],
+        in_specs=[vmem] * count,
+        out_specs=[vmem] * count,
+        scratch_shapes=buffers(nc)
+        + buffers(nz)
+        + buffers(nz)
+        + buffers(nz - 1)
+        + buffers(nz - 1)
+        + [
+            pltpu.SemaphoreType.DMA((count, nc + 2 * nz - 1)),
+            pltpu.SemaphoreType.DMA((count, nc + 2 * nz - 1)),
+        ],
+        compiler_params=pltpu.CompilerParams(
+            collective_id=5, has_side_effects=True, vmem_limit_bytes=VMEM_BYTES
+        ),
+    )(*blocks)
+
+
+def tensor_sum(part):
+    low = part.astype(jnp.bfloat16)
+    other = lax.ppermute(low, "tensor", [(0, 1), (1, 0)])
+    return low.astype(jnp.float32) + other.astype(jnp.float32)
+
+
+def head_shards(
+    layer_input,
+    segments,
+    w_qkv,
+    bias_qv,
+    w_out,
+    w_up,
+    bias_up,
+    w_down,
+    norm_gains,
+    shifts,
+    cotangent,
+):
+    rows, span, width = layer_input.shape
+    length = segments.shape[1]
+    share = w_qkv.shape[0]
+    features = w_qkv.shape[2]
+    hidden_units = w_up.shape[1]
+    nc = length // span
+    devices = 2 * nc
+    head_scale = 1.0 / math.sqrt(HEAD_DIM)
+    f32, low_type = jnp.float32, jnp.bfloat16
+    small = jnp.concatenate(
+        [norm_gains.T, shifts.T, bias_qv.reshape(share, -1), bias_up.reshape(share, -1)], axis=1
+    )
+    small = jnp.pad(small, ((0, 0), (0, 128 - small.shape[1])))
+    full_qkv, full_small, out_t, full_up, down_t = gather_weights(
+        nc, w_qkv.reshape(share, -1), small, w_out.T, w_up, w_down.T
+    )
+    gains = full_small[:, 0:2].T.astype(f32)
+    offsets = full_small[:, 2:6].T.astype(f32)
+    biases = full_small[:, 6].reshape(devices, 2, -1).transpose(1, 0, 2).reshape(2, features).astype(f32)
+    upbias = full_small[:, 7:9].reshape(-1).astype(f32)
+    bias_col = jnp.concatenate([biases[0], jnp.zeros_like(biases[0]), biases[1]])
+
+    inputs = layer_input.astype(f32)
+    normed_one, inverse_one = normalize(inputs)
+    first = (normed_one * gains[0] + offsets[0]).astype(low_type)
+    projected = jnp.einsum("dn,rcd->nrc", full_qkv, first, preferred_element_type=f32)
+    projected = (projected + bias_col[:, None, None]).astype(low_type)
+    sent = projected.reshape(3, nc, HEAD_DIM, rows, span).transpose(1, 3, 0, 2, 4)
+    qkv = exchange(sent, 1).transpose(1, 2, 3, 0, 4).reshape(rows, 3, HEAD_DIM, length)
+    queries, keys, values = qkv[:, 0], qkv[:, 1], qkv[:, 2]
+    position = jnp.arange(length, dtype=jnp.int32)
+    mask = (position[:, None] >= position[None, :])[None] & (
+        segments[:, :, None] == segments[:, None, :]
+    )
+    scores = jnp.einsum("rfi,rfj->rij", queries, keys, preferred_element_type=f32) * head_scale
+    scores = jnp.where(mask, scores, -1e30)
+    top = jnp.max(scores, axis=-1, keepdims=True)
+    exponent = jnp.exp(scores - top)
+    weights = exponent / jnp.sum(exponent, axis=-1, keepdims=True)
+    weights_low = weights.astype(low_type)
+    mixed = jnp.einsum("rfj,rij->rfi", values, weights_low, preferred_element_type=f32)
+    mixed = mixed.astype(low_type).reshape(rows, HEAD_DIM, nc, span).transpose(2, 0, 1, 3)
+    mixed = exchange(mixed, 2).transpose(1, 3, 0, 2).reshape(rows, span, features)
+
+    branch = (
+        tensor_sum(jnp.einsum("rcf,df->rcd", mixed, out_t, preferred_element_type=f32)) + offsets[2]
+    )
+    hidden = inputs + branch
+    normed_two, inverse_two = normalize(hidden)
+    second = (normed_two * gains[1] + offsets[1]).astype(low_type)
+    upward = jnp.einsum("rcd,df->rcf", second, full_up, preferred_element_type=f32) + upbias
+    active, gelu_back = jax.vjp(partial(jax.nn.gelu, approximate=True), upward)
+    active_low = active.astype(low_type)
+    down = (
+        tensor_sum(jnp.einsum("rcf,df->rcd", active_low, down_t, preferred_element_type=f32))
+        + offsets[3]
+    )
+    result = (hidden + down).astype(low_type)
+    grad_out = cotangent.astype(f32)
+    down_grad = jnp.einsum("rcd,rcf->df", cotangent, active_low, preferred_element_type=f32)
+    active_grad = jnp.einsum("rcd,df->rcf", cotangent, down_t, preferred_element_type=f32)
+    up_grad = gelu_back(active_grad)[0].astype(low_type)
+    upbias_grad = jnp.sum(up_grad, axis=(0, 1), dtype=f32)
+    second_grad = tensor_sum(
+        jnp.einsum("rcf,df->rcd", up_grad, full_up, preferred_element_type=f32)
+    )
+    upw_grad = jnp.einsum("rcd,rcf->df", second, up_grad, preferred_element_type=f32)
+    hidden_grad = grad_out + norm_back(second_grad, normed_two, inverse_two, gains[1])
+    branch_low = hidden_grad.astype(low_type)
+    mixed_grad = jnp.einsum("df,rcd->frc", out_t, branch_low, preferred_element_type=f32)
+    mixed_grad = mixed_grad.astype(low_type).reshape(nc, HEAD_DIM, rows, span).transpose(0, 2, 1, 3)
+    mixed_grad = exchange(mixed_grad, 3).transpose(1, 2, 0, 3).reshape(rows, HEAD_DIM, length)
+    outw_grad = jnp.einsum("rcd,rcf->df", branch_low, mixed, preferred_element_type=f32)
+
+    weight_grad = jnp.einsum("rfi,rfj->rij", mixed_grad, values, preferred_element_type=f32)
+    inner = jnp.sum(weights * weight_grad, axis=-1, keepdims=True)
+    score_grad = (weights * (weight_grad - inner)).astype(low_type)
+    query_grad = (
+        jnp.einsum("rfj,rij->rfi", keys, score_grad, preferred_element_type=f32) * head_scale
+    )
+    key_grad = (
+        jnp.einsum("rfi,rij->rfj", queries, score_grad, preferred_element_type=f32) * head_scale
+    )
+    value_grad = jnp.einsum("rfi,rij->rfj", mixed_grad, weights_low, preferred_element_type=f32)
+    stacked = jnp.stack([query_grad, key_grad, value_grad], axis=1).astype(low_type)
+    stacked = stacked.reshape(rows, 3, HEAD_DIM, nc, span).transpose(3, 0, 1, 2, 4)
+    stacked = exchange(stacked, 4).transpose(1, 4, 2, 0, 3).reshape(rows, span, 3 * features)
+
+    first_grad = tensor_sum(
+        jnp.einsum("rcn,dn->rcd", stacked, full_qkv, preferred_element_type=f32)
+    )
+    qkv_grad = jnp.einsum("rcd,rcn->dn", first, stacked, preferred_element_type=f32)
+    input_grad = hidden_grad + norm_back(first_grad, normed_one, inverse_one, gains[0])
+    sums = jnp.sum(stacked, axis=(0, 1), dtype=f32).reshape(3, devices, -1)
+    bias_grad = jnp.concatenate([sums[0], sums[2]], axis=1).reshape(-1, 1)
+    small_grad = jnp.concatenate(
+        [
+            jnp.stack(
+                [
+                    jnp.sum(first_grad * normed_one, axis=(0, 1)),
+                    jnp.sum(second_grad * normed_two, axis=(0, 1)),
+                    jnp.sum(first_grad, axis=(0, 1)),
+                    jnp.sum(second_grad, axis=(0, 1)),
+                    jnp.sum(branch_low, axis=(0, 1), dtype=f32),
+                    jnp.sum(cotangent, axis=(0, 1), dtype=f32),
+                ],
+                axis=1,
+            ),
+            bias_grad,
+            upbias_grad.reshape(width, -1),
+        ],
+        axis=1,
+    )
+    small_grad = jnp.pad(small_grad, ((0, 0), (0, 128 - small_grad.shape[1])))
+    sent_down, sent_up, sent_out, sent_qkv, sent_small = scatter_grads(
+        nc,
+        *[g.astype(low_type) for g in (down_grad, upw_grad, outw_grad, qkv_grad, small_grad)],
+    )
+    return (
+        result,
+        input_grad,
+        sent_qkv.reshape(w_qkv.shape),
+        sent_small[:, 6].reshape(bias_qv.shape),
+        sent_out.T,
+        sent_up,
+        sent_small[:, 7:9].reshape(bias_up.shape),
+        sent_down.T,
+        sent_small[:, 0:2].T,
+        sent_small[:, 2:6].T,
+    )
+
+
+def shards(layer_input, segments, w_qkv, *rest):
+    contexts = segments.shape[1] // layer_input.shape[1]
+    by_heads = (
+        contexts * HEAD_DIM == w_qkv.shape[2]
+        and w_qkv.shape[0] == 64
+        and layer_input.shape[1] % 128 == 0
+        and contexts % 2 == 0
+    )
+    chosen = head_shards if by_heads else general_shards
+    return chosen(layer_input, segments, w_qkv, *rest)
 
 
 def solution(mesh):

time: 1320 us -> 388 us (0.29)
  waiting for transfers between devices: 1010 us -> 20.7 us
  Pallas kernels: 0 us -> 258 us
  blocking collectives: 127 us -> 0 us
  local copies, waits for them, and re-layouts: 65 us -> 26.9 us
  matrix products: 78.5 us -> 51.9 us
  between operations: 14.6 us -> 1.17 us
    reduce_scatter x6 -> x0, waiting for transfers between devices: 544 us -> none  [the longest x2 172 us: shards(): lax.psum_scatter(extra, 'context', scatter_dimension=1, tiled=True)]
    pallas_call x0 -> x6, Pallas kernels: none -> 258 us  [the longest x1 102 us: gather_weights(): pl.pallas_call(partial(gather_kernel, count, nc // 2), out_shape=[jax.Sha...]
    unnamed x23 -> x0, waiting for transfers between devices: 207 us -> none
    all_gather x6 -> x0, waiting for transfers between devices: 179 us -> none  [the longest x1 51.1 us: shards(): lax.all_gather(w_up, ('dp', 'context'), axis=0, tiled=True)]
    all_gather x4 -> x0, blocking collectives: 127 us -> none  [the longest x1 34.4 us: shards(): lax.all_gather(shifts, ('dp', 'context'), axis=1, tiled=True)]
    psum x3 -> x0, waiting for transfers between devices: 82.6 us -> none  [the longest x1 38.6 us: shards(): lax.psum(jnp.einsum('rcf,df->rcd', up_grad, full_up, preferred_element_ty...]
    dot_general x26 -> x17, matrix products: 78.5 us -> 45.8 us  [the longest x1 5.08 us: head_shards(): jnp.einsum('rcd,rcf->df', cotangent, active_low, preferred_element_type=f32)]
    dynamic_update_slice x12 -> x0, local copies, waits for them, and re-layouts: 23.5 us -> none  [the longest x6 20.1 us: shards(): lax.map(query_side, (queries, key_rows, value_rows, query_seg, segments,...]
  transfers between devices with their start and end apart: 19 -> 4, of which waited for: 18 -> 3; matrix products, arithmetic and copies ran while one was open for 5% -> 5% of each run, Pallas kernels for 0% -> 0%
where the time goes in v1:
time: 388 us; the launch traced here: 386 us
  Pallas kernels  258 us (66%)
  matrix products  51.9 us (13%)
  local copies, waits for them, and re-layouts  26.9 us (7%)
  other arithmetic  22.6 us (6%)
  waiting for transfers between devices  20.7 us (5%)
  starting transfers between devices  5.26 us (1%)
    pallas_call x1, Pallas kernels, gather_weights(): pl.pallas_call(partial(gather_kernel, count, nc // 2), out_shape=[jax.Sha...  102 us
    pallas_call x1, Pallas kernels, scatter_grads(): pl.pallas_call(partial(scatter_kernel, count, nz), out_shape=[jax.ShapeDt...  101 us
    pallas_call x4, Pallas kernels, exchange(): pl.pallas_call(partial(exchange_kernel, nc), out_shape=jax.ShapeDtypeStru...  54.5 us
    ppermute x4, waiting for transfers between devices, tensor_sum(): other = lax.ppermute(low, 'tensor', [(0, 1), (1, 0)])  20.7 us
  transfers between devices with their start and end apart: 4, of which 3 were waited for; matrix products, arithmetic and copies ran while one was open for 5% of the time, Pallas kernels for 0%

profile of v1, /device:TPU:0, one launch (start us, length us, event | category | flops | bytes accessed | tf_op | source)
XLA Modules:
  0.0 386.4 jit_solution(3398681294219081727)
XLA Ops:
  0.6 1.6 copy.216
  2.8 1.3 reduce.30
  7.3 102.4 %shard_map.186 = (bf16[16,64,1536]{2,1,0:T(8,128)(2,1)}, bf16[16,64,128]{2,1,0:T(8,128)(2,1)}, bf16[16,64,512]{2,1,0:T(8,128)(2,1)}, bf16[16,64,2048]{2,1,0:T(8,128)(2,1)}, bf16[16,64,2048]{2,1,0:T(8,128)(2,1)}) custom-call(bf16[64,1536]{1,0:T(8,128)(2,1)} %bitcast.194, bf16[64,128]{1,0:T(8,128)(2,1)} %fusion.66.refs_1_, bf16[64,512]{1,0:T(8,128)(2,1)} %bitcast.204, ...), custom_call_target="tpu_custom_call" | custom-call | tf_op jit(solution)/shard_map/pallas_call | solution.py:330
  109.7 1.2 convert_reduce_fusion.1
  110.9 2.0 slice_convert_fusion
  112.8 1.1 slice_convert_fusion.1
  115.8 3.1 fusion.7
  118.9 0.9 copy.236
  119.8 16.8 %shard_map.187 = bf16[8,2,3,64,128]{4,3,2,1,0:T(8,128)(2,1)} custom-call(bf16[8,2,3,64,128]{4,3,2,1,0:T(8,128)(2,1)} %bitcast.177), custom_call_target="tpu_custom_call" | custom-call | tf_op jit(solution)/shard_map/pallas_call | solution.py:380
  136.6 1.7 copy.210
  138.6 6.1 %fusion.73 = (f32[2,1024]{1,0:T(2,128)S(1)}, f32[2,1024,1024]{1,2,0:T(8,128)}) fusion(s32[2,1024]{1,0:T(2,128)S(1)} %copy-done.16, pred[1024,1024]{0,1:T(8,128)(4,1)S(1)} %iota_compare_fusion, bf16[2,3,64,1024]{3,2,0,1:T(8,128)(2,1)S(1)} %reshape.237), kind=kOutput, calls=%fused_computation.133 | convolution fusion | flops 281019392 | bytes 9986048 | tf_op jit(solution)/shard_map/sub | solution.py:573
  144.6 4.3 %fusion.33 = bf16[2,8,8,8,128]{4,3,2,1,0:T(8,128)(2,1)S(1)} fusion(bf16[2,3,64,1024]{3,2,0,1:T(8,128)(2,1)S(1)} %reshape.237, f32[2,1024,1024]{1,2,0:T(8,128)} %get-tuple-element.109, f32[2,1024]{1,0:T(2,128)S(1)} %get-tuple-element.108), kind=kOutput, calls=%fused_computation.55 | convolution fusion | flops 272760832 | bytes 8921088 | tf_op jit(solution)/shard_map/rfj,rij->rfi/dot_general | solution.py:576
  149.7 13.2 %shard_map.188 = bf16[8,2,64,128]{3,2,1,0:T(8,128)(2,1)} custom-call(bf16[8,2,64,128]{3,2,1,0:T(8,128)(2,1)} %bitcast.187), custom_call_target="tpu_custom_call" | custom-call | tf_op jit(solution)/shard_map/pallas_call | solution.py:380
  163.0 1.0 copy.169
  164.5 1.6 collective-permute-start
  166.1 1.3 reshape.224
  167.4 10.0 %collective-permute-done = bf16[2,128,1024]{2,1,0:T(8,128)(2,1)S(1)} collective-permute-done((bf16[2,128,1024]{2,1,0:T(8,128)(2,1)S(1)}, bf16[2,128,1024]{2,1,0:T(8,128)(2,1)S(1)}, u32[]{:S(2)}, u32[]{:S(2)}) %collective-permute-start) | collective-permute-done | bytes 524320 | tf_op jit(solution)/shard_map/ppermute | solution.py:519
  177.4 1.4 fusion.71
  179.1 3.7 convolution_add_fusion.1
  182.8 2.3 convolution_convert_fusion.3
  185.1 1.5 collective-permute-start.1
  186.6 2.5 fusion.74
  189.1 1.4 convolution_convert_fusion.2
  191.1 3.4 bitcast_convert_fusion
  194.5 1.2 reshape.220
  195.7 1.1 copy.188
  196.8 5.1 %bitcast_convert_fusion.1 = bf16[2048,1024]{0,1:T(8,128)(2,1)} fusion(bf16[2,128,1024]{2,1,0:T(8,128)(2,1)} %param.21, f32[2,128,2048]{2,1,0:T(8,128)} %copy-done.17), kind=kOutput, calls=%fused_computation.2 | convolution fusion | flops 1080557568 | bytes 6815744 | tf_op jit(solution)/shard_map/rcd,rcf->df/dot_general | solution.py:595
  201.9 6.6 %collective-permute-done.2 = bf16[2,128,1024]{2,1,0:T(8,128)(2,1)S(1)} collective-permute-done((bf16[2,128,1024]{2,1,0:T(8,128)(2,1)S(1)}, bf16[2,128,1024]{2,1,0:T(8,128)(2,1)S(1)}, u32[]{:S(2)}, u32[]{:S(2)}) %collective-permute-start.2) | collective-permute-done | bytes 524320 | tf_op jit(solution)/shard_map/ppermute | solution.py:519
  208.5 3.0 multiply_reduce_fusion.1
  211.5 1.8 convert_reduce_fusion.2
  214.5 10.2 %shard_map.189 = bf16[8,2,64,128]{3,2,1,0:T(8,128)(2,1)} custom-call(bf16[8,2,64,128]{3,2,1,0:T(8,128)(2,1)} %bitcast.189), custom_call_target="tpu_custom_call" | custom-call | tf_op jit(solution)/shard_map/pallas_call | solution.py:380
  224.7 4.8 %multiply_reduce_fusion = (f32[2,1024]{1,0:T(2,128)S(1)}, f32[2,1024,1024]{1,2,0:T(8,128)S(1)}) fusion(f32[2,1024,1024]{1,2,0:T(8,128)} %get-tuple-element.109, f32[2,1024]{1,0:T(2,128)S(1)} %get-tuple-element.108, bf16[2,3,64,1024]{3,2,0,1:T(8,128)(2,1)S(1)} %reshape.237, bf16[8,2,64,128]{3,2,1,0:T(8,128)(2,1)} %shard_map.189), kind=kOutput, calls=%fused_computation.4 | convolution fusion | flops 274724864 | bytes 17317888 | tf_op jit(solution)/shard_map/rfi,rfj->rij/dot_general | solution.py:610
  229.5 4.6 %multiply_convert_fusion = bf16[2,1024,1024]{1,2,0:T(8,128)(2,1)S(1)} fusion(f32[2,1024,1024]{1,2,0:T(8,128)S(1)} %get-tuple-element.111, f32[2,1024]{1,0:T(2,128)S(1)} %get-tuple-element.110, f32[2,1024,1024]{1,2,0:T(8,128)} %get-tuple-element.109, f32[2,1024]{1,0:T(2,128)S(1)} %get-tuple-element.108), kind=kLoop, calls=%fused_computation.3 | loop fusion | flops 8388608 | bytes 20987904 | tf_op jit(solution)/shard_map/convert_element_type | solution.py:612
  235.0 1.4 fusion.32
  236.4 4.8 %fusion.28 = bf16[2,64,1024]{2,1,0:T(8,128)(2,1)S(1)} fusion(f32[2,1024,1024]{1,2,0:T(8,128)} %get-tuple-element.109, f32[2,1024]{1,0:T(2,128)S(1)} %get-tuple-element.108, bf16[8,2,64,128]{3,2,1,0:T(8,128)(2,1)S(1)} %copy-done.12), kind=kOutput, calls=%fused_computation.51 | convolution fusion | flops 272760832 | bytes 8921088 | tf_op jit(solution)/shard_map/rfi,rij->rfj/dot_general | solution.py:619
  241.5 1.0 maximum_bitcast_fusion.source
  242.5 14.3 %shard_map.190 = bf16[8,2,3,64,128]{4,3,2,1,0:T(8,128)(2,1)} custom-call(bf16[8,2,3,64,128]{4,3,2,1,0:T(8,128)(2,1)} %maximum_bitcast_fusion.source), custom_call_target="tpu_custom_call" | custom-call | tf_op jit(solution)/shard_map/pallas_call | solution.py:380
  256.8 1.4 bitcast_reduce_fusion
  258.6 1.2 copy.180
  259.8 3.0 convolution_convert_fusion.1
  262.8 1.6 collective-permute-start.3
  264.4 1.5 bitcast_convert_fusion.3
  265.9 2.9 bitcast_convert_fusion.2
  268.8 4.1 %collective-permute-done.3 = bf16[2,128,1024]{2,1,0:T(8,128)(2,1)S(1)} collective-permute-done((bf16[2,128,1024]{2,1,0:T(8,128)(2,1)S(1)}, bf16[2,128,1024]{2,1,0:T(8,128)(2,1)S(1)}, u32[]{:S(2)}, u32[]{:S(2)}) %collective-permute-start.3) | collective-permute-done | bytes 524320 | tf_op jit(solution)/shard_map/ppermute | solution.py:519
  274.6 101.0 %shard_map.191 = (f32[64,2048]{1,0:T(8,128)}, f32[64,2048]{1,0:T(8,128)}, f32[64,512]{1,0:T(8,128)}, f32[64,1536]{1,0:T(8,128)}, f32[64,128]{1,0:T(8,128)}) custom-call(bf16[16,64,2048]{2,1,0:T(8,128)(2,1)} %bitcast.170, bf16[16,64,2048]{2,1,0:T(8,128)(2,1)} %bitcast.167, bf16[16,64,512]{2,1,0:T(8,128)(2,1)} %bitcast.174, bf16[16,64,1536]{2,1,0:T(8,128)(2,1)} %bitcast.168, ...), custom_call_target="tpu_custom_call" | custom-call | tf_op jit(solution)/shard_map/pallas_call | solution.py:497
  377.4 0.9 slice_reduce_fusion.2
  378.4 1.8 copy.237
  382.7 1.4 fusion.41
  (100 shorter events, 19.0 us)
Async XLA Ops:
  6.6 108.7 %copy-start = (bf16[2,128,1024]{2,1,0:T(8,128)(2,1)S(1)}, bf16[2,128,1024]{2,1,0:T(8,128)(2,1)}, u32[]{:S(2)}) copy-start(bf16[2,128,1024]{2,1,0:T(8,128)(2,1)} %param.11) | copy-start | bytes 1572868
  118.9 19.7 %copy-start.16 = (s32[2,1024]{1,0:T(2,128)S(1)}, s32[2,1024]{1,0:T(2,128)}, u32[]{:S(2)}) copy-start(s32[2,1024]{1,0:T(2,128)} %param.12) | copy-start | bytes 24580
  144.6 19.3 %copy-start.1 = (bf16[16,64,512]{2,1,0:T(8,128)(2,1)S(1)}, bf16[16,64,512]{2,1,0:T(8,128)(2,1)}, u32[]{:S(2)}) copy-start(bf16[16,64,512]{2,1,0:T(8,128)(2,1)} %get-tuple-element.22) | copy-start | bytes 3145732
  164.0 13.5 %copy-start.3 = (bf16[2,128,8,64]{1,3,2,0:T(8,128)(2,1)}, bf16[2,128,8,64]{1,3,2,0:T(8,128)(2,1)S(1)}, u32[]{:S(2)}) copy-start(bf16[2,128,8,64]{1,3,2,0:T(8,128)(2,1)S(1)} %copy.169) | copy-start | bytes 786436
  164.5 12.9 %copy-start.5 = (bf16[2,128,1024]{2,1,0:T(8,128)(2,1)}, bf16[2,128,1024]{2,1,0:T(8,128)(2,1)S(1)}, u32[]{:S(2)}) copy-start(bf16[2,128,1024]{2,1,0:T(8,128)(2,1)S(1)} %convolution_convert_fusion) | copy-start | bytes 1572868
  164.5 12.9 %collective-permute-start = (bf16[2,128,1024]{2,1,0:T(8,128)(2,1)S(1)}, bf16[2,128,1024]{2,1,0:T(8,128)(2,1)S(1)}, u32[]{:S(2)}, u32[]{:S(2)}) collective-permute-start(bf16[2,128,1024]{2,1,0:T(8,128)(2,1)S(1)} %convolution_convert_fusion), channel_id=1, source_target_pairs={{0,1},{1,0},{2,3},{3,2},{4,5},{5,4},{6,7},{7,6},{8,9},{9,8},{10,11... | collective-permute-start | bytes 1572872 | tf_op jit(solution)/shard_map/ppermute | solution.py:519
  179.1 3.7 copy-start.15
  182.8 3.8 copy-start.17
  182.8 3.8 copy-start.10
  185.1 4.0 %copy-start.14 = (bf16[16,64,2048]{2,1,0:T(8,128)(2,1)S(1)}, bf16[16,64,2048]{2,1,0:T(8,128)(2,1)}, u32[]{:S(2)}) copy-start(bf16[16,64,2048]{2,1,0:T(8,128)(2,1)} %get-tuple-element.23) | copy-start | bytes 12582916
  185.1 16.8 %collective-permute-start.1 = (bf16[2,128,1024]{2,1,0:T(8,128)(2,1)}, bf16[2,128,1024]{2,1,0:T(8,128)(2,1)}, u32[]{:S(2)}, u32[]{:S(2)}) collective-permute-start(bf16[2,128,1024]{2,1,0:T(8,128)(2,1)} %convolution_convert_fusion.3), channel_id=1, source_target_pairs={{0,1},{1,0},{2,3},{3,2},{4,5},{5,4},{6,7},{7,6},{8,9},{9,8},{10,11... | collective-permute-start | bytes 1572872 | tf_op jit(solution)/shard_map/ppermute | solution.py:519
  190.5 18.0 %copy-start.6 = (bf16[2,128,1024]{2,1,0:T(8,128)(2,1)}, bf16[2,128,1024]{2,1,0:T(8,128)(2,1)S(1)}, u32[]{:S(2)}) copy-start(bf16[2,128,1024]{2,1,0:T(8,128)(2,1)S(1)} %convolution_convert_fusion.2) | copy-start | bytes 1572868
  190.5 17.9 %collective-permute-start.2 = (bf16[2,128,1024]{2,1,0:T(8,128)(2,1)S(1)}, bf16[2,128,1024]{2,1,0:T(8,128)(2,1)S(1)}, u32[]{:S(2)}, u32[]{:S(2)}) collective-permute-start(bf16[2,128,1024]{2,1,0:T(8,128)(2,1)S(1)} %convolution_convert_fusion.2), channel_id=1, source_target_pairs={{0,1},{1,0},{2,3},{3,2},{4,5},{5,4},{6,7},{7,6},{8,9},{9,8},{10,11... | collective-permute-start | bytes 1572872 | tf_op jit(solution)/shard_map/ppermute | solution.py:519
  201.9 9.6 %copy-start.11 = (bf16[2,128,1024]{2,1,0:T(8,128)(2,1)S(1)}, bf16[2,128,1024]{2,1,0:T(8,128)(2,1)}, u32[]{:S(2)}) copy-start(bf16[2,128,1024]{2,1,0:T(8,128)(2,1)} %param.21) | copy-start | bytes 1572868
  208.5 3.0 copy-start.7
  208.5 4.8 %copy-start.2 = (bf16[16,64,512]{2,1,0:T(8,128)(2,1)S(1)}, bf16[16,64,512]{2,1,0:T(8,128)(2,1)}, u32[]{:S(2)}) copy-start(bf16[16,64,512]{2,1,0:T(8,128)(2,1)} %get-tuple-element.22) | copy-start | bytes 3145732
  235.0 1.4 copy-start.12
  258.6 5.8 %copy-start.4 = (bf16[2,128,8,64]{1,3,2,0:T(8,128)(2,1)S(1)}, bf16[2,128,8,64]{1,3,2,0:T(8,128)(2,1)}, u32[]{:S(2)}) copy-start(bf16[2,128,8,64]{1,3,2,0:T(8,128)(2,1)} %copy-done.3) | copy-start | bytes 786436
  262.8 10.1 %collective-permute-start.3 = (bf16[2,128,1024]{2,1,0:T(8,128)(2,1)S(1)}, bf16[2,128,1024]{2,1,0:T(8,128)(2,1)S(1)}, u32[]{:S(2)}, u32[]{:S(2)}) collective-permute-start(bf16[2,128,1024]{2,1,0:T(8,128)(2,1)S(1)} %convolution_convert_fusion.1), channel_id=1, source_target_pairs={{0,1},{1,0},{2,3},{3,2},{4,5},{5,4},{6,7},{7,6},{8,9},{9,8},{10,11... | collective-permute-start | bytes 1572872 | tf_op jit(solution)/shard_map/ppermute | solution.py:519
  375.7 8.5 %copy-start.13 = (f32[64,512]{1,0:T(8,128)S(1)}, f32[64,512]{1,0:T(8,128)}, u32[]{:S(2)}) copy-start(f32[64,512]{1,0:T(8,128)} %get-tuple-element.27) | copy-start | bytes 393220
  375.7 9.9 %copy-start.8 = (f32[64,2048]{1,0:T(8,128)S(1)}, f32[64,2048]{1,0:T(8,128)}, u32[]{:S(2)}) copy-start(f32[64,2048]{1,0:T(8,128)} %get-tuple-element.29) | copy-start | bytes 1572868
  382.7 2.1 copy-start.9

commit v2 on v1

--- a/solution.py
+++ b/solution.py
@@ -239,6 +239,8 @@
 
 MESH = pl.DeviceIdType.MESH
 VMEM_BYTES = 56 * 1024 * 1024
+CHUNK = 1024
+AHEAD = 2
 
 
 def other_z(z, step, count):
@@ -261,81 +263,116 @@
     pl.semaphore_wait(barrier, len(peers))
 
 
-def gather_kernel(arrays, nz, *refs):
+def column_chunks(widths):
+    chunks = []
+    for a, width in enumerate(widths):
+        pieces = -(-width // CHUNK)
+        for p in range(pieces):
+            chunks.append((a, p * (width // pieces), width // pieces))
+    return chunks
+
+
+def gather_kernel(chunks, arrays, nz, *refs):
     sources, results = refs[:arrays], refs[arrays : 2 * arrays]
     own_sem, send_sem, recv_sem = refs[2 * arrays :]
     d, z, x, t = place()
     nc = 2 * nz
     here = z * 2 + x
+    mine = d * nc + here
     peer_x = (d, z * 2 + 1 - x, t)
     peer_d = (1 - d, here, t)
     peers_z = [(d, other_z(z, k, nz) * 2 + x, t) for k in range(1, nz)]
     greet(peers_z + [peer_x, peer_d])
     pending = []
 
-    def send(a, source, shard, slot, peer):
+    def source(q):
+        a, begin, size = chunks[q]
+        return sources[a].at[:, pl.ds(begin, size)]
+
+    def landing(q, shard):
+        a, begin, size = chunks[q]
+        return results[a].at[shard, :, pl.ds(begin, size)]
+
+    def send(q, origin, shard, slot, peer):
         copy = pltpu.make_async_remote_copy(
-            src_ref=source,
-            dst_ref=results[a].at[shard],
-            send_sem=send_sem.at[a, slot],
-            recv_sem=recv_sem.at[a, shard],
+            src_ref=origin,
+            dst_ref=landing(q, shard),
+            send_sem=send_sem.at[q, slot],
+            recv_sem=recv_sem.at[q, shard],
             device_id=peer,
             device_id_type=MESH,
         )
         copy.start()
         pending.append(copy)
 
-    def arrived(a, shard):
+    def arrived(q, shard):
         pltpu.make_async_remote_copy(
-            src_ref=sources[a],
-            dst_ref=results[a].at[shard],
-            send_sem=send_sem.at[a, 0],
-            recv_sem=recv_sem.at[a, shard],
+            src_ref=source(q),
+            dst_ref=landing(q, shard),
+            send_sem=send_sem.at[q, 0],
+            recv_sem=recv_sem.at[q, shard],
             device_id=peer_d,
             device_id_type=MESH,
         ).wait_recv()
 
-    mine = d * nc + here
-    locals_ = []
+    def begin_chunk(q):
+        for k in range(1, nz):
+            send(q, source(q), mine, k - 1, peers_z[k - 1])
+        send(q, source(q), mine, nz - 1, peer_x)
+        send(q, source(q), mine, 2 * nz - 1, peer_d)
+
+    def across(q):
+        for k in range(1, nz):
+            shard = d * nc + other_z(z, k, nz) * 2 + x
+            arrived(q, shard)
+            send(q, landing(q, shard), shard, nz - 1 + k, peer_x)
+            send(q, landing(q, shard), shard, 2 * nz - 1 + k, peer_d)
+
+    def inward(q):
+        for k in range(nz):
+            row = z if k == 0 else other_z(z, k, nz)
+            shard = d * nc + row * 2 + 1 - x
+            arrived(q, shard)
+            send(q, landing(q, shard), shard, 3 * nz - 1 + k, peer_d)
+
+    count = len(chunks)
+    begin_chunk(0)
+    keeps = []
     for a in range(arrays):
-        for k in range(1, nz):
-            send(a, sources[a], mine, k - 1, peers_z[k - 1])
-        send(a, sources[a], mine, nz - 1, peer_x)
-        send(a, sources[a], mine, 2 * nz - 1, peer_d)
         keep = pltpu.make_async_copy(sources[a], results[a].at[mine], own_sem.at[a])
         keep.start()
-        locals_.append(keep)
-    for a in range(arrays):
-        for k in range(nz):
-            row = z if k == 0 else other_z(z, k, nz)
-            if k:
-                shard = d * nc + row * 2 + x
-                arrived(a, shard)
-                send(a, results[a].at[shard], shard, nz - 1 + k, peer_x)
-                send(a, results[a].at[shard], shard, 2 * nz - 1 + k, peer_d)
-            shard = d * nc + row * 2 + 1 - x
-            arrived(a, shard)
-            send(a, results[a].at[shard], shard, 3 * nz - 1 + k, peer_d)
-    for a in range(arrays):
+        keeps.append(keep)
+    for q in range(1, min(AHEAD, count)):
+        begin_chunk(q)
+    for q in range(count + 1):
+        if q < count:
+            across(q)
+            if q + AHEAD < count:
+                begin_chunk(q + AHEAD)
+        if q >= 1:
+            inward(q - 1)
+    for q in range(count):
         for k in range(nc):
-            arrived(a, (1 - d) * nc + k)
-        locals_[a].wait()
+            arrived(q, (1 - d) * nc + k)
+    for keep in keeps:
+        keep.wait()
     for copy in pending:
         copy.wait_send()
 
 
 def gather_weights(nc, *arrays):
     count = len(arrays)
+    chunks = column_chunks([a.shape[1] for a in arrays])
     hbm = pl.BlockSpec(memory_space=pl.ANY)
     results = pl.pallas_call(
-        partial(gather_kernel, count, nc // 2),
+        partial(gather_kernel, chunks, count, nc // 2),
         out_shape=[jax.ShapeDtypeStruct((2 * nc,) + a.shape, a.dtype) for a in arrays],
         in_specs=[hbm] * count,
         out_specs=[hbm] * count,
         scratch_shapes=[
             pltpu.SemaphoreType.DMA((count,)),
-            pltpu.SemaphoreType.DMA((count, 2 * nc - 1)),
-            pltpu.SemaphoreType.DMA((count, 2 * nc)),
+            pltpu.SemaphoreType.DMA((len(chunks), 2 * nc - 1)),
+            pltpu.SemaphoreType.DMA((len(chunks), 2 * nc)),
         ],
         compiler_params=pltpu.CompilerParams(collective_id=0, has_side_effects=True),
     )(*arrays)
@@ -391,11 +428,12 @@
     )(blocks)
 
 
-def scatter_kernel(arrays, nz, *refs):
+def scatter_kernel(chunks, arrays, nz, *refs):
     grads, results = refs[:arrays], refs[arrays : 2 * arrays]
     scratch = refs[2 * arrays :]
-    from_d, to_x, from_x, to_z, from_z = (scratch[i * arrays : (i + 1) * arrays] for i in range(5))
-    send_sem, recv_sem = scratch[5 * arrays :]
+    count = len(chunks)
+    from_d, to_x, from_x, to_z, from_z = (scratch[i * count : (i + 1) * count] for i in range(5))
+    send_sem, recv_sem = scratch[5 * count :]
     d, z, x, t = place()
     nc = 2 * nz
     here = z * 2 + x
@@ -406,12 +444,16 @@
     greet(peers_z + [peer_x, peer_d])
     pending = []
 
-    def send(a, source, target, slot, peer):
+    def grad(q, shard):
+        a, begin, size = chunks[q]
+        return grads[a].at[shard, :, pl.ds(begin, size)]
+
+    def send(q, source, target, slot, peer):
         copy = pltpu.make_async_remote_copy(
             src_ref=source,
             dst_ref=target,
-            send_sem=send_sem.at[a, slot],
-            recv_sem=recv_sem.at[a, slot],
+            send_sem=send_sem.at[q, slot],
+            recv_sem=recv_sem.at[q, slot],
             device_id=peer,
             device_id_type=MESH,
         )
@@ -431,55 +473,66 @@
             target[part] = total.astype(target.dtype)
 
     order = list(range(1, nz)) + [0]
-    halves = [[], []]
-    for a in range(arrays):
-        first = {}
+    first, second, third = {}, {}, {}
+
+    def inward(q):
         for side in range(2):
             for k in order:
                 column = 1 - x if side == 0 else x
-                shard = rows[k] * 2 + column
                 slot = side * nz + k
-                first[slot] = send(
-                    a, grads[a].at[(1 - d) * nc + shard], from_d[a].at[slot], slot, peer_d
+                first[q, slot] = send(
+                    q,
+                    grad(q, (1 - d) * nc + rows[k] * 2 + column),
+                    from_d[q].at[slot],
+                    slot,
+                    peer_d,
                 )
-        halves[0].append(first)
-    for a in range(arrays):
-        second = {}
+
+    def across(q):
         for k in order:
-            halves[0][a][k].wait_recv()
-            added(
-                to_x[a].at[k], grads[a].at[d * nc + rows[k] * 2 + 1 - x], from_d[a].at[k]
-            )
-            second[k] = send(a, to_x[a].at[k], from_x[a].at[k], nc + k, peer_x)
-        halves[1].append(second)
-    last = []
-    for a in range(arrays):
-        third = []
+            first[q, k].wait_recv()
+            added(to_x[q].at[k], grad(q, d * nc + rows[k] * 2 + 1 - x), from_d[q].at[k])
+            second[q, k] = send(q, to_x[q].at[k], from_x[q].at[k], nc + k, peer_x)
+
+    def along(q):
         for k in order:
-            halves[0][a][nz + k].wait_recv()
-            halves[1][a][k].wait_recv()
+            first[q, nz + k].wait_recv()
+            second[q, k].wait_recv()
             if k:
                 added(
-                    to_z[a].at[k - 1],
-                    grads[a].at[d * nc + rows[k] * 2 + x],
-                    from_d[a].at[nz + k],
-                    from_x[a].at[k],
+                    to_z[q].at[k - 1],
+                    grad(q, d * nc + rows[k] * 2 + x),
+                    from_d[q].at[nz + k],
+                    from_x[q].at[k],
                 )
                 back = (nz - k) if nz != 4 else k
-                third.append(
-                    send(a, to_z[a].at[k - 1], from_z[a].at[back - 1], nc + nz + k - 1, peers_z[k - 1])
+                third[q, back] = send(
+                    q, to_z[q].at[k - 1], from_z[q].at[back - 1], nc + nz + back - 1, peers_z[k - 1]
                 )
-        last.append(third)
-    for a in range(arrays):
-        for copy in last[a]:
-            copy.wait_recv()
+
+    def finish(q):
+        for k in range(1, nz):
+            third[q, k].wait_recv()
+        a, begin, size = chunks[q]
         added(
-            results[a],
-            grads[a].at[d * nc + here],
-            from_d[a].at[nz],
-            from_x[a].at[0],
-            *[from_z[a].at[k] for k in range(nz - 1)],
-        )
+            results[a].at[:, pl.ds(begin, size)],
+            grad(q, d * nc + here),
+            from_d[q].at[nz],
+            from_x[q].at[0],
+            *[from_z[q].at[k] for k in range(nz - 1)],
+        )
+
+    for q in range(min(AHEAD, count)):
+        inward(q)
+    for q in range(count + 4):
+        if q + AHEAD < count:
+            inward(q + AHEAD)
+        if q < count:
+            across(q)
+        if 0 <= q - 2 < count:
+            along(q - 2)
+        if 0 <= q - 4 < count:
+            finish(q - 4)
     for copy in pending:
         copy.wait_send()
 
@@ -488,15 +541,16 @@
     count = len(arrays)
     nz = nc // 2
     blocks = [a.reshape((2 * nc, -1, a.shape[-1])) for a in arrays]
-    shapes = [b.shape[1:] for b in blocks]
+    share = blocks[0].shape[1]
+    chunks = column_chunks([b.shape[2] for b in blocks])
     vmem = pl.BlockSpec(memory_space=pltpu.VMEM)
 
     def buffers(number):
-        return [pltpu.VMEM((number,) + s, jnp.bfloat16) for s in shapes]
+        return [pltpu.VMEM((number, share, size), jnp.bfloat16) for _, _, size in chunks]
 
     return pl.pallas_call(
-        partial(scatter_kernel, count, nz),
-        out_shape=[jax.ShapeDtypeStruct(s, jnp.float32) for s in shapes],
+        partial(scatter_kernel, chunks, count, nz),
+        out_shape=[jax.ShapeDtypeStruct(b.shape[1:], jnp.float32) for b in blocks],
         in_specs=[vmem] * count,
         out_specs=[vmem] * count,
         scratch_shapes=buffers(nc)
@@ -505,8 +559,8 @@
         + buffers(nz - 1)
         + buffers(nz - 1)
         + [
-            pltpu.SemaphoreType.DMA((count, nc + 2 * nz - 1)),
-            pltpu.SemaphoreType.DMA((count, nc + 2 * nz - 1)),
+            pltpu.SemaphoreType.DMA((len(chunks), nc + 2 * nz - 1)),
+            pltpu.SemaphoreType.DMA((len(chunks), nc + 2 * nz - 1)),
         ],
         compiler_params=pltpu.CompilerParams(
             collective_id=5, has_side_effects=True, vmem_limit_bytes=VMEM_BYTES

time: 388 us -> 367 us (0.946)
  Pallas kernels: 258 us -> 240 us
    pallas_call x2, Pallas kernels: 203 us -> 184 us  [the longest x1 97.1 us: scatter_grads(): pl.pallas_call(partial(scatter_kernel, chunks, count, nz), out_shape=[jax...]
  transfers between devices with their start and end apart: 4 -> 4, of which waited for: 3 -> 3; matrix products, arithmetic and copies ran while one was open for 5% -> 6% of each run, Pallas kernels for 0% -> 0%
where the time goes in v2:
time: 367 us; the launch traced here: 366 us
  Pallas kernels  240 us (65%)
  matrix products  51.9 us (14%)
  local copies, waits for them, and re-layouts  26.9 us (7%)
  other arithmetic  22.6 us (6%)
  waiting for transfers between devices  18 us (5%)
  starting transfers between devices  5.29 us (1%)
    pallas_call x1, Pallas kernels, scatter_grads(): pl.pallas_call(partial(scatter_kernel, chunks, count, nz), out_shape=[jax...  97.1 us
    pallas_call x1, Pallas kernels, gather_weights(): pl.pallas_call(partial(gather_kernel, chunks, count, nc // 2), out_shape=...  87.2 us
    pallas_call x4, Pallas kernels, exchange(): pl.pallas_call(partial(exchange_kernel, nc), out_shape=jax.ShapeDtypeStru...  55.7 us
    ppermute x4, waiting for transfers between devices, tensor_sum(): other = lax.ppermute(low, 'tensor', [(0, 1), (1, 0)])  18 us
  transfers between devices with their start and end apart: 4, of which 3 were waited for; matrix products, arithmetic and copies ran while one was open for 6% of the time, Pallas kernels for 0%

profile of v2, /device:TPU:0, one launch (start us, length us, event | category | flops | bytes accessed | tf_op | source)
XLA Modules:
  0.0 365.8 jit_solution(9060274028951669885)
XLA Ops:
  0.6 1.6 copy.216
  2.8 1.3 reduce.30
  7.3 87.2 %shard_map.186 = (bf16[16,64,1536]{2,1,0:T(8,128)(2,1)}, bf16[16,64,128]{2,1,0:T(8,128)(2,1)}, bf16[16,64,512]{2,1,0:T(8,128)(2,1)}, bf16[16,64,2048]{2,1,0:T(8,128)(2,1)}, bf16[16,64,2048]{2,1,0:T(8,128)(2,1)}) custom-call(bf16[64,1536]{1,0:T(8,128)(2,1)} %bitcast.194, bf16[64,128]{1,0:T(8,128)(2,1)} %fusion.66.refs_1_, bf16[64,512]{1,0:T(8,128)(2,1)} %bitcast.204, ...), custom_call_target="tpu_custom_call" | custom-call | tf_op jit(solution)/shard_map/pallas_call | solution.py:367
  94.5 1.2 convert_reduce_fusion.1
  95.7 2.0 slice_convert_fusion
  97.6 1.1 slice_convert_fusion.1
  100.5 3.1 fusion.7
  103.7 0.9 copy.236
  104.6 18.4 %shard_map.187 = bf16[8,2,3,64,128]{4,3,2,1,0:T(8,128)(2,1)} custom-call(bf16[8,2,3,64,128]{4,3,2,1,0:T(8,128)(2,1)} %bitcast.177), custom_call_target="tpu_custom_call" | custom-call | tf_op jit(solution)/shard_map/pallas_call | solution.py:417
  123.0 1.7 copy.210
  125.0 6.1 %fusion.73 = (f32[2,1024]{1,0:T(2,128)S(1)}, f32[2,1024,1024]{1,2,0:T(8,128)}) fusion(s32[2,1024]{1,0:T(2,128)S(1)} %copy-done.16, pred[1024,1024]{0,1:T(8,128)(4,1)S(1)} %iota_compare_fusion, bf16[2,3,64,1024]{3,2,0,1:T(8,128)(2,1)S(1)} %reshape.237), kind=kOutput, calls=%fused_computation.133 | convolution fusion | flops 281019392 | bytes 9986048 | tf_op jit(solution)/shard_map/sub | solution.py:627
  131.0 4.3 %fusion.33 = bf16[2,8,8,8,128]{4,3,2,1,0:T(8,128)(2,1)S(1)} fusion(bf16[2,3,64,1024]{3,2,0,1:T(8,128)(2,1)S(1)} %reshape.237, f32[2,1024,1024]{1,2,0:T(8,128)} %get-tuple-element.109, f32[2,1024]{1,0:T(2,128)S(1)} %get-tuple-element.108), kind=kOutput, calls=%fused_computation.55 | convolution fusion | flops 272760832 | bytes 8921088 | tf_op jit(solution)/shard_map/rfj,rij->rfi/dot_general | solution.py:630
  136.1 13.4 %shard_map.188 = bf16[8,2,64,128]{3,2,1,0:T(8,128)(2,1)} custom-call(bf16[8,2,64,128]{3,2,1,0:T(8,128)(2,1)} %bitcast.187), custom_call_target="tpu_custom_call" | custom-call | tf_op jit(solution)/shard_map/pallas_call | solution.py:417
  149.5 1.0 copy.169
  151.0 1.6 collective-permute-start
  152.6 1.3 reshape.224
  153.9 9.1 %collective-permute-done = bf16[2,128,1024]{2,1,0:T(8,128)(2,1)S(1)} collective-permute-done((bf16[2,128,1024]{2,1,0:T(8,128)(2,1)S(1)}, bf16[2,128,1024]{2,1,0:T(8,128)(2,1)S(1)}, u32[]{:S(2)}, u32[]{:S(2)}) %collective-permute-start) | collective-permute-done | bytes 524320 | tf_op jit(solution)/shard_map/ppermute | solution.py:573
  163.0 1.4 fusion.71
  164.7 3.7 %convolution_add_fusion.1 = f32[2,128,2048]{2,1,0:T(8,128)S(1)} fusion(bf16[1024,2048,1]{1,0,2:T(8,128)(2,1)} %bitcast.213, f32[2048]{0:T(1024)S(1)} %reshape.224, f32[2,128,1024]{2,1,0:T(8,128)S(1)} %get-tuple-element.97, f32[1024]{0:T(1024)S(1)} %bitcast.202, f32[1024]{0:T(1024)S(1)} %get-tuple-element.88, f32[2,128]{1,0:T(2,128)S(1)} %add_rsqrt_fusion, ...), kind=kOutput, calls=%fused_computation.20 | convolution fusion | flops 1075576832 | bytes 7358464 | tf_op jit(solution)/shard_map/rcd,df->rcf/dot_general | solution.py:640
  168.4 2.3 convolution_convert_fusion.3
  170.7 1.6 collective-permute-start.1
  172.2 2.5 fusion.74
  174.7 1.4 convolution_convert_fusion.2
  176.7 3.4 bitcast_convert_fusion
  180.1 1.2 reshape.220
  181.3 1.1 copy.188
  182.4 5.1 %bitcast_convert_fusion.1 = bf16[2048,1024]{0,1:T(8,128)(2,1)} fusion(bf16[2,128,1024]{2,1,0:T(8,128)(2,1)} %param.21, f32[2,128,2048]{2,1,0:T(8,128)} %copy-done.17), kind=kOutput, calls=%fused_computation.2 | convolution fusion | flops 1080557568 | bytes 6815744 | tf_op jit(solution)/shard_map/rcd,rcf->df/dot_general | solution.py:649
  187.5 5.6 %collective-permute-done.2 = bf16[2,128,1024]{2,1,0:T(8,128)(2,1)S(1)} collective-permute-done((bf16[2,128,1024]{2,1,0:T(8,128)(2,1)S(1)}, bf16[2,128,1024]{2,1,0:T(8,128)(2,1)S(1)}, u32[]{:S(2)}, u32[]{:S(2)}) %collective-permute-start.2) | collective-permute-done | bytes 524320 | tf_op jit(solution)/shard_map/ppermute | solution.py:573
  193.1 3.0 multiply_reduce_fusion.1
  196.1 1.8 convert_reduce_fusion.2
  199.2 10.3 %shard_map.189 = bf16[8,2,64,128]{3,2,1,0:T(8,128)(2,1)} custom-call(bf16[8,2,64,128]{3,2,1,0:T(8,128)(2,1)} %bitcast.189), custom_call_target="tpu_custom_call" | custom-call | tf_op jit(solution)/shard_map/pallas_call | solution.py:417
  209.5 4.8 %multiply_reduce_fusion = (f32[2,1024]{1,0:T(2,128)S(1)}, f32[2,1024,1024]{1,2,0:T(8,128)S(1)}) fusion(f32[2,1024,1024]{1,2,0:T(8,128)} %get-tuple-element.109, f32[2,1024]{1,0:T(2,128)S(1)} %get-tuple-element.108, bf16[2,3,64,1024]{3,2,0,1:T(8,128)(2,1)S(1)} %reshape.237, bf16[8,2,64,128]{3,2,1,0:T(8,128)(2,1)} %shard_map.189), kind=kOutput, calls=%fused_computation.4 | convolution fusion | flops 274724864 | bytes 17317888 | tf_op jit(solution)/shard_map/rfi,rfj->rij/dot_general | solution.py:664
  214.3 4.6 %multiply_convert_fusion = bf16[2,1024,1024]{1,2,0:T(8,128)(2,1)S(1)} fusion(f32[2,1024,1024]{1,2,0:T(8,128)S(1)} %get-tuple-element.111, f32[2,1024]{1,0:T(2,128)S(1)} %get-tuple-element.110, f32[2,1024,1024]{1,2,0:T(8,128)} %get-tuple-element.109, f32[2,1024]{1,0:T(2,128)S(1)} %get-tuple-element.108), kind=kLoop, calls=%fused_computation.3 | loop fusion | flops 8388608 | bytes 20987904 | tf_op jit(solution)/shard_map/convert_element_type | solution.py:666
  219.9 1.4 fusion.32
  221.3 4.8 %fusion.28 = bf16[2,64,1024]{2,1,0:T(8,128)(2,1)S(1)} fusion(f32[2,1024,1024]{1,2,0:T(8,128)} %get-tuple-element.109, f32[2,1024]{1,0:T(2,128)S(1)} %get-tuple-element.108, bf16[8,2,64,128]{3,2,1,0:T(8,128)(2,1)S(1)} %copy-done.12), kind=kOutput, calls=%fused_computation.51 | convolution fusion | flops 272760832 | bytes 8921088 | tf_op jit(solution)/shard_map/rfi,rij->rfj/dot_general | solution.py:673
  226.3 1.0 maximum_bitcast_fusion.source
  227.3 13.6 %shard_map.190 = bf16[8,2,3,64,128]{4,3,2,1,0:T(8,128)(2,1)} custom-call(bf16[8,2,3,64,128]{4,3,2,1,0:T(8,128)(2,1)} %maximum_bitcast_fusion.source), custom_call_target="tpu_custom_call" | custom-call | tf_op jit(solution)/shard_map/pallas_call | solution.py:417
  240.9 1.4 bitcast_reduce_fusion
  242.7 1.2 copy.180
  244.0 2.9 convolution_convert_fusion.1
  246.9 1.6 collective-permute-start.3
  248.6 1.5 bitcast_convert_fusion.3
  250.1 2.9 bitcast_convert_fusion.2
  252.9 3.3 collective-permute-done.3
  258.0 97.1 %shard_map.191 = (f32[64,2048]{1,0:T(8,128)}, f32[64,2048]{1,0:T(8,128)}, f32[64,512]{1,0:T(8,128)}, f32[64,1536]{1,0:T(8,128)}, f32[64,128]{1,0:T(8,128)}) custom-call(bf16[16,64,2048]{2,1,0:T(8,128)(2,1)} %bitcast.170, bf16[16,64,2048]{2,1,0:T(8,128)(2,1)} %bitcast.167, bf16[16,64,512]{2,1,0:T(8,128)(2,1)} %bitcast.174, bf16[16,64,1536]{2,1,0:T(8,128)(2,1)} %bitcast.168, ...), custom_call_target="tpu_custom_call" | custom-call | tf_op jit(solution)/shard_map/pallas_call | solution.py:551
  356.9 0.9 slice_reduce_fusion.2
  357.8 1.8 copy.237
  362.2 1.4 fusion.41
  (100 shorter events, 19.0 us)
Async XLA Ops:
  6.6 93.5 %copy-start = (bf16[2,128,1024]{2,1,0:T(8,128)(2,1)S(1)}, bf16[2,128,1024]{2,1,0:T(8,128)(2,1)}, u32[]{:S(2)}) copy-start(bf16[2,128,1024]{2,1,0:T(8,128)(2,1)} %param.11) | copy-start | bytes 1572868
  103.6 21.3 %copy-start.16 = (s32[2,1024]{1,0:T(2,128)S(1)}, s32[2,1024]{1,0:T(2,128)}, u32[]{:S(2)}) copy-start(s32[2,1024]{1,0:T(2,128)} %param.12) | copy-start | bytes 24580
  131.0 19.5 %copy-start.1 = (bf16[16,64,512]{2,1,0:T(8,128)(2,1)S(1)}, bf16[16,64,512]{2,1,0:T(8,128)(2,1)}, u32[]{:S(2)}) copy-start(bf16[16,64,512]{2,1,0:T(8,128)(2,1)} %get-tuple-element.22) | copy-start | bytes 3145732
  150.5 12.5 %copy-start.3 = (bf16[2,128,8,64]{1,3,2,0:T(8,128)(2,1)}, bf16[2,128,8,64]{1,3,2,0:T(8,128)(2,1)S(1)}, u32[]{:S(2)}) copy-start(bf16[2,128,8,64]{1,3,2,0:T(8,128)(2,1)S(1)} %copy.169) | copy-start | bytes 786436
  151.0 12.0 %copy-start.5 = (bf16[2,128,1024]{2,1,0:T(8,128)(2,1)}, bf16[2,128,1024]{2,1,0:T(8,128)(2,1)S(1)}, u32[]{:S(2)}) copy-start(bf16[2,128,1024]{2,1,0:T(8,128)(2,1)S(1)} %convolution_convert_fusion) | copy-start | bytes 1572868
  151.0 12.0 %collective-permute-start = (bf16[2,128,1024]{2,1,0:T(8,128)(2,1)S(1)}, bf16[2,128,1024]{2,1,0:T(8,128)(2,1)S(1)}, u32[]{:S(2)}, u32[]{:S(2)}) collective-permute-start(bf16[2,128,1024]{2,1,0:T(8,128)(2,1)S(1)} %convolution_convert_fusion), channel_id=1, source_target_pairs={{0,1},{1,0},{2,3},{3,2},{4,5},{5,4},{6,7},{7,6},{8,9},{9,8},{10,11... | collective-permute-start | bytes 1572872 | tf_op jit(solution)/shard_map/ppermute | solution.py:573
  164.7 3.7 %copy-start.15 = (bf16[16,64,2048]{2,1,0:T(8,128)(2,1)S(1)}, bf16[16,64,2048]{2,1,0:T(8,128)(2,1)}, u32[]{:S(2)}) copy-start(bf16[16,64,2048]{2,1,0:T(8,128)(2,1)} %get-tuple-element.24) | copy-start | bytes 12582916
  168.4 3.9 %copy-start.17 = (f32[2,128,2048]{2,1,0:T(8,128)}, f32[2,128,2048]{2,1,0:T(8,128)S(1)}, u32[]{:S(2)}) copy-start(f32[2,128,2048]{2,1,0:T(8,128)S(1)} %convolution_add_fusion.1) | copy-start | bytes 6291460
  168.4 3.8 %copy-start.10 = (bf16[2,128,1024]{2,1,0:T(8,128)(2,1)S(1)}, bf16[2,128,1024]{2,1,0:T(8,128)(2,1)}, u32[]{:S(2)}) copy-start(bf16[2,128,1024]{2,1,0:T(8,128)(2,1)} %param.21) | copy-start | bytes 1572868
  170.7 4.1 %copy-start.14 = (bf16[16,64,2048]{2,1,0:T(8,128)(2,1)S(1)}, bf16[16,64,2048]{2,1,0:T(8,128)(2,1)}, u32[]{:S(2)}) copy-start(bf16[16,64,2048]{2,1,0:T(8,128)(2,1)} %get-tuple-element.23) | copy-start | bytes 12582916
  170.7 16.8 %collective-permute-start.1 = (bf16[2,128,1024]{2,1,0:T(8,128)(2,1)}, bf16[2,128,1024]{2,1,0:T(8,128)(2,1)}, u32[]{:S(2)}, u32[]{:S(2)}) collective-permute-start(bf16[2,128,1024]{2,1,0:T(8,128)(2,1)} %convolution_convert_fusion.3), channel_id=1, source_target_pairs={{0,1},{1,0},{2,3},{3,2},{4,5},{5,4},{6,7},{7,6},{8,9},{9,8},{10,11... | collective-permute-start | bytes 1572872 | tf_op jit(solution)/shard_map/ppermute | solution.py:573
  176.1 17.0 %copy-start.6 = (bf16[2,128,1024]{2,1,0:T(8,128)(2,1)}, bf16[2,128,1024]{2,1,0:T(8,128)(2,1)S(1)}, u32[]{:S(2)}) copy-start(bf16[2,128,1024]{2,1,0:T(8,128)(2,1)S(1)} %convolution_convert_fusion.2) | copy-start | bytes 1572868
  176.1 16.9 %collective-permute-start.2 = (bf16[2,128,1024]{2,1,0:T(8,128)(2,1)S(1)}, bf16[2,128,1024]{2,1,0:T(8,128)(2,1)S(1)}, u32[]{:S(2)}, u32[]{:S(2)}) collective-permute-start(bf16[2,128,1024]{2,1,0:T(8,128)(2,1)S(1)} %convolution_convert_fusion.2), channel_id=1, source_target_pairs={{0,1},{1,0},{2,3},{3,2},{4,5},{5,4},{6,7},{7,6},{8,9},{9,8},{10,11... | collective-permute-start | bytes 1572872 | tf_op jit(solution)/shard_map/ppermute | solution.py:573
  187.5 8.6 %copy-start.11 = (bf16[2,128,1024]{2,1,0:T(8,128)(2,1)S(1)}, bf16[2,128,1024]{2,1,0:T(8,128)(2,1)}, u32[]{:S(2)}) copy-start(bf16[2,128,1024]{2,1,0:T(8,128)(2,1)} %param.21) | copy-start | bytes 1572868
  193.1 3.0 copy-start.7
  193.1 4.8 %copy-start.2 = (bf16[16,64,512]{2,1,0:T(8,128)(2,1)S(1)}, bf16[16,64,512]{2,1,0:T(8,128)(2,1)}, u32[]{:S(2)}) copy-start(bf16[16,64,512]{2,1,0:T(8,128)(2,1)} %get-tuple-element.22) | copy-start | bytes 3145732
  219.8 1.4 copy-start.12
  242.7 5.8 %copy-start.4 = (bf16[2,128,8,64]{1,3,2,0:T(8,128)(2,1)S(1)}, bf16[2,128,8,64]{1,3,2,0:T(8,128)(2,1)}, u32[]{:S(2)}) copy-start(bf16[2,128,8,64]{1,3,2,0:T(8,128)(2,1)} %copy-done.3) | copy-start | bytes 786436
  246.9 9.3 %collective-permute-start.3 = (bf16[2,128,1024]{2,1,0:T(8,128)(2,1)S(1)}, bf16[2,128,1024]{2,1,0:T(8,128)(2,1)S(1)}, u32[]{:S(2)}, u32[]{:S(2)}) collective-permute-start(bf16[2,128,1024]{2,1,0:T(8,128)(2,1)S(1)} %convolution_convert_fusion.1), channel_id=1, source_target_pairs={{0,1},{1,0},{2,3},{3,2},{4,5},{5,4},{6,7},{7,6},{8,9},{9,8},{10,11... | collective-permute-start | bytes 1572872 | tf_op jit(solution)/shard_map/ppermute | solution.py:573
  355.1 8.5 %copy-start.13 = (f32[64,512]{1,0:T(8,128)S(1)}, f32[64,512]{1,0:T(8,128)}, u32[]{:S(2)}) copy-start(f32[64,512]{1,0:T(8,128)} %get-tuple-element.27) | copy-start | bytes 393220
  355.1 9.9 %copy-start.8 = (f32[64,2048]{1,0:T(8,128)S(1)}, f32[64,2048]{1,0:T(8,128)}, u32[]{:S(2)}) copy-start(f32[64,2048]{1,0:T(8,128)} %get-tuple-element.29) | copy-start | bytes 1572868
  362.2 2.1 copy-start.9
